TPU v7x, 32 devices: a whole 2x2x4 slice. The times are simulated.
32 devices in a mesh: section: 4 (over y, x), dp: 8 (over z, core).
Axes of the slice: x: 2, y: 2, z: 4, core: 2. Of those that a mesh axis runs over, the one named last changes fastest.
Arguments:
- images: bfloat16 [4, 8, 8, 24, 512], P(None, 'dp')
- image_group: int32 [4, 8], P(None, 'dp'), may hold values from 0 to 2, as said below
- group_size: int32 [3, 2], replicated, may hold values from 4 to 24, as said below
- conv_weight: bfloat16 [4, 512, 3, 3, 512], P('section'), may hold values from -0.09375 to 0.09375
- bn_gain: float32 [4, 512], P('section'), may hold values from 0.1 to 1.9
- bn_bias: float32 [4, 512], P('section'), may hold values from -3 to 3
- cotangent: bfloat16 [4, 8, 8, 24, 512], P(None, 'dp'), may hold values from -6 to 6
Outputs:
- activations: bfloat16 [4, 8, 8, 24, 512], P('section', 'dp')
- input_grad: bfloat16 [4, 8, 8, 24, 512], P('section', 'dp')
- weight_grad: float32 [4, 512, 3, 3, 512], P('section', 'dp')
- gain_grad: float32 [4, 512], P('section', 'dp')
- bias_grad: float32 [4, 512], P('section', 'dp')
Inputs may be any that keep to these rules, and one draw needn't show every extreme that they name: `image_group`: in every micro-batch some image is of group 0. `group_size`: row g holds the height and the width of group g; group 0 fills the canvas, 8 by 24; heights are at least 4 and widths at least 12.
All inputs are finite; a program needn't handle non-finite values.
Results may differ from a plain program's by a relative error of at most 0.04.
Values may be sent and summed in bfloat16 or wider, within the bound.
No kernel may reach another device: no remote copies, remote signals or barrier semaphores. Data moves between devices by JAX's collectives and lax.ppermute only.
A program may use at most 256 MiB of HBM per device.

v0:
```python
from functools import partial

import jax
import jax.numpy as jnp
from jax import lax
from jax.sharding import PartitionSpec as P

CONVS = 2


eps = 1e-05


def from_behind(x, axis, by):
    peers = lax.axis_size(axis)
    pairs = [(i, i + by) for i in range(peers) if 0 <= i + by < peers]
    return lax.ppermute(x, axis, pairs)


def canvas_mask(image_group, group_size, canvas_rows, canvas_cols):
    groups_n = group_size.shape[0]
    onehot = image_group[..., None] == jnp.arange(groups_n, dtype=jnp.int32)
    height = jnp.sum(jnp.where(onehot, group_size[:, 0], 0), axis=-1)
    breadth = jnp.sum(jnp.where(onehot, group_size[:, 1], 0), axis=-1)
    inside_rows = jnp.arange(canvas_rows, dtype=jnp.int32)[:, None] < height[..., None, None]
    inside_cols = jnp.arange(canvas_cols, dtype=jnp.int32)[None, :] < breadth[..., None, None]
    return (inside_rows & inside_cols).astype(jnp.float32)[..., None]


def window_pool(hidden):
    frames, height, breadth, channels = hidden.shape
    blocks = hidden.reshape(frames, height // 2, 2, breadth // 2, 2, channels)
    window_max = jnp.max(blocks, axis=(2, 4), keepdims=True)
    raised = jnp.exp(blocks - window_max)
    weights = raised / jnp.sum(raised, axis=(2, 4), keepdims=True)
    pooled = jnp.sum(weights * blocks, axis=(2, 4), keepdims=True)
    return (weights * pooled).reshape(frames, height, breadth, channels)


def activate(pre_act, inside, pooling):
    hidden = jax.nn.silu(pre_act) * inside
    return jnp.where(pooling, window_pool(hidden) * inside, hidden)


def conv_forward(layer_in, weight):
    return lax.conv_general_dilated(
        layer_in,
        weight,
        (1, 1),
        "SAME",
        dimension_numbers=("NHWC", "IHWO", "NHWC"),
        preferred_element_type=jnp.float32,
    )


def conv_data_back(grad_pre, weight):
    flipped = weight[:, ::-1, ::-1, :]
    return lax.conv_general_dilated(
        grad_pre,
        flipped,
        (1, 1),
        "SAME",
        dimension_numbers=("NHWC", "OHWI", "NHWC"),
        preferred_element_type=jnp.float32,
    )


def weight_back(layer_in, grad_pre):
    height = layer_in.shape[1]
    breadth = layer_in.shape[2]
    padded = jnp.pad(layer_in, ((0, 0), (1, 1), (1, 1), (0, 0)))
    pieces = []
    for tap_row in range(3):
        for tap_col in range(3):
            window = padded[:, tap_row : tap_row + height, tap_col : tap_col + breadth, :]
            pieces.append(
                jnp.einsum("nhwi,nhwo->io", window, grad_pre, preferred_element_type=jnp.float32)
            )
    return jnp.stack(pieces, axis=1).reshape(layer_in.shape[3], 3, 3, grad_pre.shape[3])


def layer_forward(layer_in, weight, gain_row, bias_row, inside, pooling):
    pre_norm = conv_forward(layer_in, weight)
    sums = lax.psum(
        (
            jnp.sum(pre_norm * inside, axis=(0, 1, 2)),
            jnp.sum(pre_norm * pre_norm * inside, axis=(0, 1, 2)),
            jnp.sum(inside),
        ),
        "dp",
    )
    pixel_total = sums[2]
    mean_val = sums[0] / pixel_total
    scale_inv = lax.rsqrt(sums[1] / pixel_total - mean_val * mean_val + eps)
    pre_act = (pre_norm - mean_val) * scale_inv * gain_row + bias_row
    hidden = activate(pre_act, inside, pooling)
    return (pre_norm, mean_val, scale_inv, pixel_total, hidden)


def layer_backward(
    grad_out,
    layer_in,
    pre_norm,
    mean_val,
    scale_inv,
    pixel_total,
    weight,
    gain_row,
    bias_row,
    inside,
    pooling,
):
    normed = (pre_norm - mean_val) * scale_inv
    pre_act = normed * gain_row + bias_row
    hidden_out, pullback = jax.vjp(partial(activate, inside=inside, pooling=pooling), pre_act)
    grad_act = pullback(grad_out)[0]
    sums = lax.psum(
        (jnp.sum(grad_act, axis=(0, 1, 2)), jnp.sum(grad_act * normed, axis=(0, 1, 2))), "dp"
    )
    shift_term = sums[0] / pixel_total
    slope_term = sums[1] / pixel_total
    grad_pre = (
        inside * scale_inv * gain_row * (grad_act - shift_term - normed * slope_term)
    ).astype(jnp.bfloat16)
    weight_term = weight_back(layer_in, grad_pre)
    grad_in = conv_data_back(grad_pre, weight).astype(jnp.bfloat16)
    return (grad_in, weight_term, sums[1], sums[0])


def shards(images, image_group, group_size, conv_weight, bn_gain, bn_bias, cotangent):
    section_index = lax.axis_index("section")
    sections = lax.axis_size("section")
    micro_total = images.shape[0]
    channels = conv_weight.shape[1]
    inside_all = canvas_mask(image_group, group_size, images.shape[2], images.shape[3])
    ticks = micro_total + sections - 1
    weight = conv_weight[0]
    gain_row = bn_gain[0]
    bias_row = bn_bias[0]
    pool_here = section_index == CONVS - 1
    received = jnp.zeros(images.shape[1:], jnp.bfloat16)
    kept_in, kept_pre, kept_mean, kept_scale, kept_total, finished = ([], [], [], [], [], [])
    for tick in range(ticks):
        micro_pos = jnp.clip(tick - section_index, 0, micro_total - 1)
        inside = inside_all[micro_pos]
        fresh = (images[micro_pos].astype(jnp.float32) * inside).astype(jnp.bfloat16)
        layer_in = jnp.where(section_index == 0, fresh, received)
        pre_norm, mean_val, scale_inv, pixel_total, hidden = layer_forward(
            layer_in, weight, gain_row, bias_row, inside, pool_here
        )
        sent = hidden.astype(jnp.bfloat16)
        if tick < ticks - 1:
            received = from_behind(sent, "section", 1)
        kept_in.append(layer_in)
        kept_pre.append(pre_norm)
        kept_mean.append(mean_val)
        kept_scale.append(scale_inv)
        kept_total.append(pixel_total)
        finished.append(sent)
    stack_in = jnp.stack(kept_in)
    stack_pre = jnp.stack(kept_pre)
    stack_mean = jnp.stack(kept_mean)
    stack_scale = jnp.stack(kept_scale)
    stack_total = jnp.stack(kept_total)
    returned = jnp.zeros(images.shape[1:], jnp.bfloat16)
    weight_sum = jnp.zeros(conv_weight.shape[1:], jnp.float32)
    gain_sum = jnp.zeros((channels,), jnp.float32)
    bias_sum = jnp.zeros((channels,), jnp.float32)
    input_list = []
    for tick in range(ticks):
        micro_raw = tick - (sections - 1 - section_index)
        valid = ((micro_raw >= 0) & (micro_raw < micro_total)).astype(jnp.float32)
        micro_pos = jnp.clip(micro_raw, 0, micro_total - 1)
        forward_tick = jnp.clip(micro_pos + section_index, 0, ticks - 1)
        inside = inside_all[micro_pos]
        grad_out = jnp.where(
            section_index == sections - 1,
            cotangent[micro_pos].astype(jnp.float32),
            returned.astype(jnp.float32),
        )
        grad_in, weight_term, gain_term, bias_term = layer_backward(
            grad_out,
            stack_in[forward_tick],
            stack_pre[forward_tick],
            stack_mean[forward_tick],
            stack_scale[forward_tick],
            stack_total[forward_tick],
            weight,
            gain_row,
            bias_row,
            inside,
            pool_here,
        )
        weight_sum = weight_sum + valid * weight_term
        gain_sum = gain_sum + valid * gain_term
        bias_sum = bias_sum + valid * bias_term
        if tick < ticks - 1:
            returned = from_behind(grad_in, "section", -1)
        input_list.append((grad_in.astype(jnp.float32) * inside).astype(jnp.bfloat16))
    out_stack = jnp.stack(finished[sections - 1 :], axis=0)
    grad_stack = jnp.stack(input_list[sections - 1 :], axis=0)
    out_back, grad_back = (
        lax.all_to_all(out_stack, "section", split_axis=0, concat_axis=1, tiled=True),
        lax.all_to_all(grad_stack, "section", split_axis=0, concat_axis=1, tiled=True),
    )
    activations = out_back[:, sections - 1 : sections]
    input_grad = grad_back[:, 0:1]
    weight_grad = lax.psum_scatter(weight_sum[None], "dp", scatter_dimension=1, tiled=True)
    share = channels // lax.axis_size("dp")
    gain_grad = lax.dynamic_slice_in_dim(gain_sum, lax.axis_index("dp") * share, share)[None]
    bias_grad = lax.dynamic_slice_in_dim(bias_sum, lax.axis_index("dp") * share, share)[None]
    return (activations, input_grad, weight_grad, gain_grad, bias_grad)


def solution(mesh):
    in_specs = (
        P(None, "dp", None, None, None),
        P(None, "dp"),
        P(),
        P("section", None, None, None, None),
        P("section", None),
        P("section", None),
        P(None, "dp", None, None, None),
    )
    out_specs = (
        P("section", "dp", None, None, None),
        P("section", "dp", None, None, None),
        P("section", "dp", None, None, None),
        P("section", "dp"),
        P("section", "dp"),
    )
    return jax.shard_map(shards, mesh=mesh, in_specs=in_specs, out_specs=out_specs, check_vma=False)
```

profile of v0, /device:TPU:0, one launch (start us, length us, event | category | flops | bytes accessed | tf_op | source)
XLA Modules:
  0.0 874.8 jit_solution(16265183276298841896)
XLA Ops:
  9.0 2.3 constant_dynamic-slice_fusion.43
  13.1 3.7 fusion.766
  17.7 19.0 %all-reduce.20 = (f32[512]{0:T(512)S(1)}, f32[]{:T(128)}, f32[512]{0:T(512)S(1)}) all-reduce(f32[512]{0:T(512)S(1)} %fusion.266, f32[]{:T(128)} %get-tuple-element.60, f32[512]{0:T(512)S(1)} %fusion.358), channel_id=1, replica_groups=mesh['section'=4,'dp'=8] {'dp'}, use_global_device_ids=true, to_apply=%region_7.8 | all-reduce | flops 1025 | bytes 8200 | tf_op jit(solution)/shard_map/psum | solution.py:84
  46.7 3.4 collective-permute-start
  64.7 3.7 fusion.767
  69.4 14.6 %all-reduce.19 = (f32[512]{0:T(512)S(1)}, f32[]{:T(128)}, f32[512]{0:T(512)S(1)}) all-reduce(f32[512]{0:T(512)S(1)} %fusion.264, f32[]{:T(128)} %get-tuple-element.61, f32[512]{0:T(512)S(1)} %fusion.352), channel_id=1, replica_groups=mesh['section'=4,'dp'=8] {'dp'}, use_global_device_ids=true, to_apply=%region_16.17 | all-reduce | flops 1025 | bytes 8200 | tf_op jit(solution)/shard_map/psum | solution.py:84
  94.5 3.4 collective-permute-start.1
  99.5 2.4 collective-permute-done.1
  103.0 3.7 fusion.768
  107.6 14.5 %all-reduce.18 = (f32[512]{0:T(512)S(1)}, f32[]{:T(128)}, f32[512]{0:T(512)S(1)}) all-reduce(f32[512]{0:T(512)S(1)} %fusion.262, f32[]{:T(128)} %get-tuple-element.62, f32[512]{0:T(512)S(1)} %fusion.346), channel_id=1, replica_groups=mesh['section'=4,'dp'=8] {'dp'}, use_global_device_ids=true, to_apply=%region_25.26 | all-reduce | flops 1025 | bytes 8200 | tf_op jit(solution)/shard_map/psum | solution.py:84
  132.7 4.6 collective-permute-start.2
  138.9 2.2 collective-permute-done.2
  142.2 3.7 fusion.769
  146.8 14.4 %all-reduce.17 = (f32[512]{0:T(512)S(1)}, f32[]{:T(128)}, f32[512]{0:T(512)S(1)}) all-reduce(f32[512]{0:T(512)S(1)} %fusion.260, f32[]{:T(128)} %get-tuple-element.63, f32[512]{0:T(512)S(1)} %fusion.340), channel_id=1, replica_groups=mesh['section'=4,'dp'=8] {'dp'}, use_global_device_ids=true, to_apply=%region_34.35 | all-reduce | flops 1025 | bytes 8200 | tf_op jit(solution)/shard_map/psum | solution.py:84
  169.2 4.4 collective-permute-start.3
  178.7 3.7 fusion.770
  183.2 14.8 %all-reduce.16 = (f32[512]{0:T(512)S(1)}, f32[]{:T(128)}, f32[512]{0:T(512)S(1)}) all-reduce(f32[512]{0:T(512)S(1)} %fusion.258, f32[]{:T(128)} %get-tuple-element.59, f32[512]{0:T(512)S(1)} %fusion.334), channel_id=1, replica_groups=mesh['section'=4,'dp'=8] {'dp'}, use_global_device_ids=true, to_apply=%region_43.44 | all-reduce | flops 1025 | bytes 8200 | tf_op jit(solution)/shard_map/psum | solution.py:84
  204.6 5.2 collective-permute-start.4
  211.3 2.5 collective-permute-done.4
  214.2 3.7 fusion.771
  218.8 14.5 %all-reduce.15 = (f32[512]{0:T(512)S(1)}, f32[]{:T(128)}, f32[512]{0:T(512)S(1)}) all-reduce(f32[512]{0:T(512)S(1)} %fusion.256, f32[]{:T(128)} %get-tuple-element.58, f32[512]{0:T(512)S(1)} %fusion.328), channel_id=1, replica_groups=mesh['section'=4,'dp'=8] {'dp'}, use_global_device_ids=true, to_apply=%region_52.53 | all-reduce | flops 1025 | bytes 8200 | tf_op jit(solution)/shard_map/psum | solution.py:84
  239.8 5.3 collective-permute-start.5
  246.8 2.4 collective-permute-done.5
  249.6 3.7 fusion.772
  258.6 14.7 %all-reduce.14 = (f32[512]{0:T(512)S(1)}, f32[]{:T(128)}, f32[512]{0:T(512)S(1)}) all-reduce(f32[512]{0:T(512)S(1)} %fusion.254, f32[]{:T(128)} %get-tuple-element.57, f32[512]{0:T(512)S(1)} %fusion.322), channel_id=1, replica_groups=mesh['section'=4,'dp'=8] {'dp'}, use_global_device_ids=true, to_apply=%region_61.62 | all-reduce | flops 1025 | bytes 8200 | tf_op jit(solution)/shard_map/psum | solution.py:84
  275.3 6.2 fusion.751
  285.7 2.8 multiply_reduce_fusion.31
  305.5 4.6 stack.394
  312.5 2.4 constant_dynamic-slice_fusion.6
  318.6 4.0 fusion.759
  354.4 3.6 fusion.743
  357.9 14.3 %all-reduce.13 = (f32[512]{0:T(512)}, f32[512]{0:T(512)}) all-reduce(f32[512]{0:T(512)} %get-tuple-element.54, f32[512]{0:T(512)} %get-tuple-element.53), channel_id=1, replica_groups=mesh['section'=4,'dp'=8] {'dp'}, use_global_device_ids=true, to_apply=%region_75.76 | all-reduce | flops 1024 | bytes 8192 | tf_op jit(solution)/shard_map/psum | solution.py:117
  376.4 3.8 fusion.154
  405.9 2.3 fusion.539
  408.2 2.3 fusion.90
  410.5 2.2 fusion.89
  433.5 2.5 multiply_reduce_fusion.26
  448.5 2.2 broadcast_in_dim.289
  450.7 3.7 fusion.742
  454.4 14.3 %all-reduce.12 = (f32[512]{0:T(512)}, f32[512]{0:T(512)}) all-reduce(f32[512]{0:T(512)} %get-tuple-element.50, f32[512]{0:T(512)} %get-tuple-element.49), channel_id=1, replica_groups=mesh['section'=4,'dp'=8] {'dp'}, use_global_device_ids=true, to_apply=%region_86.87 | all-reduce | flops 1024 | bytes 8192 | tf_op jit(solution)/shard_map/psum | solution.py:117
  473.8 3.8 fusion.151
  498.7 2.3 multiply_reduce_fusion.21
  508.6 2.9 fusion.741
  511.5 14.5 %all-reduce.11 = (f32[512]{0:T(512)}, f32[512]{0:T(512)}) all-reduce(f32[512]{0:T(512)} %get-tuple-element.46, f32[512]{0:T(512)} %get-tuple-element.45), channel_id=1, replica_groups=mesh['section'=4,'dp'=8] {'dp'}, use_global_device_ids=true, to_apply=%region_97.98 | all-reduce | flops 1024 | bytes 8192 | tf_op jit(solution)/shard_map/psum | solution.py:117
  530.6 3.8 fusion.148
  554.5 2.2 multiply_reduce_fusion.16
  563.5 2.8 fusion.740
  566.3 14.1 %all-reduce.10 = (f32[512]{0:T(512)S(1)}, f32[512]{0:T(512)S(1)}) all-reduce(f32[512]{0:T(512)} %get-tuple-element.42, f32[512]{0:T(512)} %get-tuple-element.41), channel_id=1, replica_groups=mesh['section'=4,'dp'=8] {'dp'}, use_global_device_ids=true, to_apply=%region_108.109 | all-reduce | flops 1024 | bytes 8192 | tf_op jit(solution)/shard_map/psum | solution.py:117
  583.4 3.8 fusion.145
  588.7 2.2 fusion.63
  612.9 13.9 %all-reduce.9 = (f32[512]{0:T(512)S(1)}, f32[512]{0:T(512)S(1)}) all-reduce(f32[512]{0:T(512)S(1)} %get-tuple-element.38, f32[512]{0:T(512)S(1)} %get-tuple-element.37), channel_id=1, replica_groups=mesh['section'=4,'dp'=8] {'dp'}, use_global_device_ids=true, to_apply=%region_119.120 | all-reduce | flops 1024 | bytes 8192 | tf_op jit(solution)/shard_map/psum | solution.py:117
  629.9 3.8 fusion.142
  658.2 13.9 %all-reduce.8 = (f32[512]{0:T(512)S(1)}, f32[512]{0:T(512)S(1)}) all-reduce(f32[512]{0:T(512)S(1)} %get-tuple-element.34, f32[512]{0:T(512)S(1)} %get-tuple-element.33), channel_id=1, replica_groups=mesh['section'=4,'dp'=8] {'dp'}, use_global_device_ids=true, to_apply=%region_130.131 | all-reduce | flops 1024 | bytes 8192 | tf_op jit(solution)/shard_map/psum | solution.py:117
  675.3 3.8 fusion.139
  701.2 13.8 %all-reduce.7 = (f32[512]{0:T(512)S(1)}, f32[512]{0:T(512)S(1)}) all-reduce(f32[512]{0:T(512)S(1)} %get-tuple-element.30, f32[512]{0:T(512)S(1)} %get-tuple-element.29), channel_id=1, replica_groups=mesh['section'=4,'dp'=8] {'dp'}, use_global_device_ids=true, to_apply=%region_141.142 | all-reduce | flops 1024 | bytes 8192 | tf_op jit(solution)/shard_map/psum | solution.py:117
  719.8 2.3 fusion.36
  722.0 2.2 fusion.35
  724.3 2.2 fusion.34
  734.6 26.8 %add_add_fusion = f32[512,9,512]{2,0,1:T(8,128)} fusion(f32[512,9,512]{2,0,1:T(8,128)} %fusion.28, f32[512,9,512]{2,0,1:T(8,128)} %fusion.37, f32[512,9,512]{2,0,1:T(8,128)} %fusion.46, f32[512,9,512]{2,0,1:T(8,128)} %fusion.55, f32[512,9,512]{2,0,1:T(8,128)} %fusion.64, f32[512,9,512]{2,0,1:T(8,128)} %fusion.73, f32[512,9,512]{2,0,1:T(8,128)} %fusion.82, ...), kind=kLoop, calls=%fused_computation | loop fusion | flops 30670848 | bytes 75497504 | tf_op jit(solution)/shard_map/add | solution.py:194
  770.2 12.2 %all-to-all-start = ((bf16[4,1,8,24,512]{4,2,3,1,0:T(8,128)(2,1)}), bf16[4,1,8,24,512]{4,2,3,1,0:T(8,128)(2,1)S(1)}, u32[]{:S(2)}, u32[]{:S(2)}) async-start(bf16[4,1,8,24,512]{4,2,3,1,0:T(8,128)(2,1)} %pad_maximum_fusion), calls=%async_computation | async-start | bytes 1572864 | tf_op jit(solution)/shard_map/all_to_all | solution.py:203
  786.6 3.8 fusion.136
  793.2 3.5 all-to-all-start.1
  800.0 7.1 all-to-all-done.1
  807.9 59.6 %reduce-scatter.2.cloned.1.call-done = f32[1,64,3,3,512]{4,1,3,2,0:T(8,128)} async-done(((f32[1,512,3,3,512]{4,1,3,2,0:T(8,128)}), f32[1,64,3,3,512]{4,1,3,2,0:T(8,128)}) %reduce-scatter.2.cloned.1.call-update) | async-done | bytes 1179664 | tf_op jit(solution)/shard_map/reduce_scatter | solution.py:208
  (865 shorter events, 393.4 us)
Async XLA Ops:
  7.2 30.2 %copy-start.104 = (f32[1,512]{1,0:T(1,128)S(1)}, f32[1,512]{1,0:T(1,128)}, u32[]{:S(2)}) copy-start(f32[1,512]{1,0:T(1,128)} %param.12) | copy-start | bytes 6148
  7.2 30.2 %copy-start.28 = (f32[1,512]{1,0:T(1,128)S(1)}, f32[1,512]{1,0:T(1,128)}, u32[]{:S(2)}) copy-start(f32[1,512]{1,0:T(1,128)} %param.11) | copy-start | bytes 6148
  7.2 860.3 %reduce-scatter.2.cloned.1.call-start = ((), (), s32[]{:S(2)}) async-start(), calls=%async_computation.3 | async-start | bytes 10616832 | tf_op jit(solution)/shard_map/reduce_scatter | solution.py:208
  11.3 237.9 %copy-start.29 = (bf16[1,1,8,24,512]{4,3,2,1,0:T(8,128)(2,1)}, bf16[1,1,8,24,512]{4,3,2,1,0:T(8,128)(2,1)S(1)}, u32[]{:S(2)}) copy-start(bf16[1,1,8,24,512]{4,3,2,1,0:T(8,128)(2,1)S(1)} %get-tuple-element.143) | copy-start | bytes 589828
  12.7 298.1 %copy-start.64 = (f32[8,24]{0,1:T(8,128)}, f32[8,24]{0,1:T(8,128)S(1)}, u32[]{:S(2)}) copy-start(f32[8,24]{0,1:T(8,128)S(1)} %get-tuple-element.162) | copy-start | bytes 2308
  16.8 44.0 %copy-start.25 = (bf16[4,1,8,24,512]{4,3,2,1,0:T(8,128)(2,1)S(1)}, bf16[4,1,8,24,512]{4,3,2,1,0:T(8,128)(2,1)}, u32[]{:S(2)}) copy-start(bf16[4,1,8,24,512]{4,3,2,1,0:T(8,128)(2,1)} %param.13) | copy-start | bytes 2359300
  37.4 27.3 %copy-start.142 = (f32[512]{0:T(512)}, f32[512]{0:T(512)S(1)}, u32[]{:S(2)}) copy-start(f32[512]{0:T(512)S(1)} %get-tuple-element.204) | copy-start | bytes 6148
  39.2 24.4 %copy-start.32 = (bf16[1,1,8,24,512]{4,3,2,1,0:T(8,128)(2,1)S(1)}, bf16[1,1,8,24,512]{4,3,2,1,0:T(8,128)(2,1)}, u32[]{:S(2)}) copy-start(bf16[1,1,8,24,512]{4,3,2,1,0:T(8,128)(2,1)} %get-tuple-element.147) | copy-start | bytes 589828
  46.7 22.1 %copy-start.69 = (f32[8,24]{0,1:T(8,128)S(1)}, f32[8,24]{0,1:T(8,128)}, u32[]{:S(2)}) copy-start(f32[8,24]{0,1:T(8,128)} %get-tuple-element.161) | copy-start | bytes 2308
  46.7 16.3 %collective-permute-start = (bf16[1,8,24,512]{3,1,2,0:T(8,128)(2,1)S(1)}, bf16[1,8,24,512]{3,1,2,0:T(8,128)(2,1)S(1)}, u32[]{:S(2)}, u32[]{:S(2)}) collective-permute-start(bf16[1,8,24,512]{3,1,2,0:T(8,128)(2,1)S(1)} %fusion.353), channel_id=1, source_target_pairs={{0,8},{8,16},{16,24},{1,9},{9,17},{17,25},{2,10},{10,18},{18,26},{... | collective-permute-start | bytes 589832 | tf_op jit(solution)/shard_map/ppermute | solution.py:17
  61.9 23.3 %copy-start.14 = (bf16[1,1,8,24,512]{4,3,2,1,0:T(8,128)(2,1)}, bf16[1,1,8,24,512]{4,3,2,1,0:T(8,128)(2,1)S(1)}, u32[]{:S(2)}) copy-start(bf16[1,1,8,24,512]{4,3,2,1,0:T(8,128)(2,1)S(1)} %get-tuple-element.139) | copy-start | bytes 589828
  64.7 28.5 %copy-start.70 = (f32[8,24]{0,1:T(8,128)S(1)}, f32[8,24]{0,1:T(8,128)}, u32[]{:S(2)}) copy-start(f32[8,24]{0,1:T(8,128)} %get-tuple-element.161) | copy-start | bytes 2308
  68.5 30.3 %copy-start.33 = (bf16[1,1,8,24,512]{4,3,2,1,0:T(8,128)(2,1)S(1)}, bf16[1,1,8,24,512]{4,3,2,1,0:T(8,128)(2,1)}, u32[]{:S(2)}) copy-start(bf16[1,1,8,24,512]{4,3,2,1,0:T(8,128)(2,1)} %get-tuple-element.147) | copy-start | bytes 589828
  68.5 34.2 %copy-start.31 = (bf16[1,1,8,24,512]{4,3,2,1,0:T(8,128)(2,1)S(1)}, bf16[1,1,8,24,512]{4,3,2,1,0:T(8,128)(2,1)}, u32[]{:S(2)}) copy-start(bf16[1,1,8,24,512]{4,3,2,1,0:T(8,128)(2,1)} %get-tuple-element.148) | copy-start | bytes 589828
  68.5 34.2 %copy-start.68 = (f32[8,24]{0,1:T(8,128)S(1)}, f32[8,24]{0,1:T(8,128)}, u32[]{:S(2)}) copy-start(f32[8,24]{0,1:T(8,128)} %get-tuple-element.160) | copy-start | bytes 2308
  68.5 34.5 %copy-start.174 = (pred[8,4]{0,1:T(4,128)(4,1)S(1)}, pred[8,4]{0,1:T(4,128)(4,1)}, u32[]{:S(2)}) copy-start(pred[8,4]{0,1:T(4,128)(4,1)} %constant.167) | copy-start | bytes 100
  84.6 22.2 %copy-start.146 = (f32[512]{0:T(512)}, f32[512]{0:T(512)S(1)}, u32[]{:S(2)}) copy-start(f32[512]{0:T(512)S(1)} %get-tuple-element.202) | copy-start | bytes 6148
  84.6 22.2 %copy-start.148 = (f32[512]{0:T(512)}, f32[512]{0:T(512)S(1)}, u32[]{:S(2)}) copy-start(f32[512]{0:T(512)S(1)} %get-tuple-element.203) | copy-start | bytes 6148
  94.5 7.4 collective-permute-start.1
  106.8 35.1 %copy-start.30 = (bf16[1,1,8,24,512]{4,3,2,1,0:T(8,128)(2,1)S(1)}, bf16[1,1,8,24,512]{4,3,2,1,0:T(8,128)(2,1)}, u32[]{:S(2)}) copy-start(bf16[1,1,8,24,512]{4,3,2,1,0:T(8,128)(2,1)} %get-tuple-element.149) | copy-start | bytes 589828
  106.8 35.0 %copy-start.67 = (f32[8,24]{0,1:T(8,128)S(1)}, f32[8,24]{0,1:T(8,128)}, u32[]{:S(2)}) copy-start(f32[8,24]{0,1:T(8,128)} %get-tuple-element.159) | copy-start | bytes 2308
  122.8 23.1 %copy-start.150 = (f32[512]{0:T(512)}, f32[512]{0:T(512)S(1)}, u32[]{:S(2)}) copy-start(f32[512]{0:T(512)S(1)} %get-tuple-element.200) | copy-start | bytes 6148
  122.8 23.1 %copy-start.152 = (f32[512]{0:T(512)}, f32[512]{0:T(512)S(1)}, u32[]{:S(2)}) copy-start(f32[512]{0:T(512)S(1)} %get-tuple-element.201) | copy-start | bytes 6148
  132.7 8.4 collective-permute-start.2
  145.9 32.4 %copy-start.66 = (f32[8,24]{0,1:T(8,128)S(1)}, f32[8,24]{0,1:T(8,128)}, u32[]{:S(2)}) copy-start(f32[8,24]{0,1:T(8,128)} %get-tuple-element.158) | copy-start | bytes 2308
  169.2 8.4 collective-permute-start.3
  204.6 30.3 %copy-start.86 = (bf16[1,8,24,512]{3,1,2,0:T(8,128)(2,1)}, bf16[1,8,24,512]{3,1,2,0:T(8,128)(2,1)S(1)}, u32[]{:S(2)}) copy-start(bf16[1,8,24,512]{3,1,2,0:T(8,128)(2,1)S(1)} %fusion.329) | copy-start | bytes 589828
  204.6 9.3 %collective-permute-start.4 = (bf16[1,8,24,512]{3,1,2,0:T(8,128)(2,1)S(1)}, bf16[1,8,24,512]{3,1,2,0:T(8,128)(2,1)S(1)}, u32[]{:S(2)}, u32[]{:S(2)}) collective-permute-start(bf16[1,8,24,512]{3,1,2,0:T(8,128)(2,1)S(1)} %fusion.329), channel_id=1, source_target_pairs={{0,8},{8,16},{16,24},{1,9},{9,17},{17,25},{2,10},{10,18},{18,26},{... | collective-permute-start | bytes 589832 | tf_op jit(solution)/shard_map/ppermute | solution.py:17
  213.8 20.7 %copy-start.93 = (bf16[1,8,24,512]{3,1,2,0:T(8,128)(2,1)}, bf16[1,8,24,512]{3,1,2,0:T(8,128)(2,1)S(1)}, u32[]{:S(2)}) copy-start(bf16[1,8,24,512]{3,1,2,0:T(8,128)(2,1)S(1)} %collective-permute-done.4) | copy-start | bytes 589828
  217.9 31.6 %copy-start.175 = (pred[8,4]{0,1:T(4,128)(4,1)S(1)}, pred[8,4]{0,1:T(4,128)(4,1)}, u32[]{:S(2)}) copy-start(pred[8,4]{0,1:T(4,128)(4,1)} %constant.167) | copy-start | bytes 100
  239.8 9.4 %collective-permute-start.5 = (bf16[1,8,24,512]{3,1,2,0:T(8,128)(2,1)S(1)}, bf16[1,8,24,512]{3,1,2,0:T(8,128)(2,1)S(1)}, u32[]{:S(2)}, u32[]{:S(2)}) collective-permute-start(bf16[1,8,24,512]{3,1,2,0:T(8,128)(2,1)S(1)} %fusion.323), channel_id=1, source_target_pairs={{0,8},{8,16},{16,24},{1,9},{9,17},{17,25},{2,10},{10,18},{18,26},{... | collective-permute-start | bytes 589832 | tf_op jit(solution)/shard_map/ppermute | solution.py:17
  253.3 20.6 %copy-start.145 = (f32[512]{0:T(512)S(1)}, f32[512]{0:T(512)}, u32[]{:S(2)}) copy-start(f32[512]{0:T(512)} %copy-done.144) | copy-start | bytes 6148
  253.3 20.6 %copy-start.149 = (f32[512]{0:T(512)S(1)}, f32[512]{0:T(512)}, u32[]{:S(2)}) copy-start(f32[512]{0:T(512)} %copy-done.148) | copy-start | bytes 6148
  253.3 20.6 %copy-start.153 = (f32[512]{0:T(512)S(1)}, f32[512]{0:T(512)}, u32[]{:S(2)}) copy-start(f32[512]{0:T(512)} %copy-done.152) | copy-start | bytes 6148
  253.4 20.6 %copy-start.157 = (f32[512]{0:T(512)S(1)}, f32[512]{0:T(512)}, u32[]{:S(2)}) copy-start(f32[512]{0:T(512)} %copy-done.156) | copy-start | bytes 6148
  253.4 21.2 %copy-start.143 = (f32[512]{0:T(512)S(1)}, f32[512]{0:T(512)}, u32[]{:S(2)}) copy-start(f32[512]{0:T(512)} %copy-done.142) | copy-start | bytes 6148
  253.4 21.1 %copy-start.147 = (f32[512]{0:T(512)S(1)}, f32[512]{0:T(512)}, u32[]{:S(2)}) copy-start(f32[512]{0:T(512)} %copy-done.146) | copy-start | bytes 6148
  253.4 21.1 %copy-start.151 = (f32[512]{0:T(512)S(1)}, f32[512]{0:T(512)}, u32[]{:S(2)}) copy-start(f32[512]{0:T(512)} %copy-done.150) | copy-start | bytes 6148
  253.4 21.1 %copy-start.155 = (f32[512]{0:T(512)S(1)}, f32[512]{0:T(512)}, u32[]{:S(2)}) copy-start(f32[512]{0:T(512)} %copy-done.154) | copy-start | bytes 6148
  253.4 21.1 %copy-start.159 = (f32[512]{0:T(512)S(1)}, f32[512]{0:T(512)}, u32[]{:S(2)}) copy-start(f32[512]{0:T(512)} %copy-done.158) | copy-start | bytes 6148
  253.4 21.1 %copy-start.163 = (f32[512]{0:T(512)S(1)}, f32[512]{0:T(512)}, u32[]{:S(2)}) copy-start(f32[512]{0:T(512)} %copy-done.162) | copy-start | bytes 6148
  254.6 44.4 %copy-start.1 = (f32[1,1,8,24,512]{4,2,3,1,0:T(8,128)}, f32[1,1,8,24,512]{4,2,3,1,0:T(8,128)S(1)}, u32[]{:S(2)}) copy-start(f32[1,1,8,24,512]{4,2,3,1,0:T(8,128)S(1)} %get-tuple-element.128) | copy-start | bytes 1179652
  312.5 41.8 %copy-start.105 = (f32[1,512]{1,0:T(1,128)S(1)}, f32[1,512]{1,0:T(1,128)}, u32[]{:S(2)}) copy-start(f32[1,512]{1,0:T(1,128)} %param.12) | copy-start | bytes 6148
  312.5 41.8 %copy-start.133 = (f32[1,512]{1,0:T(1,128)S(1)}, f32[1,512]{1,0:T(1,128)}, u32[]{:S(2)}) copy-start(f32[1,512]{1,0:T(1,128)} %copy-done.132) | copy-start | bytes 6148
  312.5 41.8 %copy-start.135 = (f32[1,512]{1,0:T(1,128)S(1)}, f32[1,512]{1,0:T(1,128)}, u32[]{:S(2)}) copy-start(f32[1,512]{1,0:T(1,128)} %copy-done.134) | copy-start | bytes 6148
  381.0 44.5 %collective-permute-start.6 = (bf16[1,8,24,512]{3,1,2,0:T(8,128)(2,1)}, bf16[1,8,24,512]{3,1,2,0:T(8,128)(2,1)}, u32[]{:S(2)}, u32[]{:S(2)}) collective-permute-start(bf16[1,8,24,512]{3,1,2,0:T(8,128)(2,1)} %slice_bitcast_fusion.5), channel_id=1, source_target_pairs={{8,0},{16,8},{24,16},{9,1},{17,9},{25,17},{10,2},{18,10},{26,18},{... | collective-permute-start | bytes 589832 | tf_op jit(solution)/shard_map/ppermute | solution.py:17
  420.9 29.8 %copy-start.2 = (f32[1,1,8,24,512]{4,2,3,1,0:T(8,128)S(1)}, f32[1,1,8,24,512]{4,2,3,1,0:T(8,128)}, u32[]{:S(2)}) copy-start(f32[1,1,8,24,512]{4,2,3,1,0:T(8,128)} %copy-done.1) | copy-start | bytes 1179652
  420.9 29.8 %copy-start.127 = (f32[1,512]{1,0:T(1,128)S(1)}, f32[1,512]{1,0:T(1,128)}, u32[]{:S(2)}) copy-start(f32[1,512]{1,0:T(1,128)} %copy-done.126) | copy-start | bytes 6148
  420.9 29.8 %copy-start.129 = (f32[1,512]{1,0:T(1,128)S(1)}, f32[1,512]{1,0:T(1,128)}, u32[]{:S(2)}) copy-start(f32[1,512]{1,0:T(1,128)} %copy-done.128) | copy-start | bytes 6148
  477.8 13.4 %collective-permute-start.7 = (bf16[1,8,24,512]{3,1,2,0:T(8,128)(2,1)S(1)}, bf16[1,8,24,512]{3,1,2,0:T(8,128)(2,1)S(1)}, u32[]{:S(2)}, u32[]{:S(2)}) collective-permute-start(bf16[1,8,24,512]{3,1,2,0:T(8,128)(2,1)S(1)} %slice_bitcast_fusion.4), channel_id=1, source_target_pairs={{8,0},{16,8},{24,16},{9,1},{17,9},{25,17},{10,2},{18,10},{26,18},{... | collective-permute-start | bytes 589832 | tf_op jit(solution)/shard_map/ppermute | solution.py:17
  534.6 13.3 %collective-permute-start.8 = (bf16[1,8,24,512]{3,1,2,0:T(8,128)(2,1)S(1)}, bf16[1,8,24,512]{3,1,2,0:T(8,128)(2,1)S(1)}, u32[]{:S(2)}, u32[]{:S(2)}) collective-permute-start(bf16[1,8,24,512]{3,1,2,0:T(8,128)(2,1)S(1)} %slice_bitcast_fusion.3), channel_id=1, source_target_pairs={{8,0},{16,8},{24,16},{9,1},{17,9},{25,17},{10,2},{18,10},{26,18},{... | collective-permute-start | bytes 589832 | tf_op jit(solution)/shard_map/ppermute | solution.py:17
  587.4 14.3 %collective-permute-start.9 = (bf16[1,8,24,512]{3,1,2,0:T(8,128)(2,1)S(1)}, bf16[1,8,24,512]{3,1,2,0:T(8,128)(2,1)S(1)}, u32[]{:S(2)}, u32[]{:S(2)}) collective-permute-start(bf16[1,8,24,512]{3,1,2,0:T(8,128)(2,1)S(1)} %slice_bitcast_fusion.2), channel_id=1, source_target_pairs={{8,0},{16,8},{24,16},{9,1},{17,9},{25,17},{10,2},{18,10},{26,18},{... | collective-permute-start | bytes 589832 | tf_op jit(solution)/shard_map/ppermute | solution.py:17
  612.9 22.3 %copy-start.115 = (bf16[1,8,24,512]{3,2,1,0:T(8,128)(2,1)S(1)}, bf16[1,8,24,512]{3,2,1,0:T(8,128)(2,1)}, u32[]{:S(2)}) copy-start(bf16[1,8,24,512]{3,2,1,0:T(8,128)(2,1)} %get-tuple-element.238) | copy-start | bytes 589828
  633.9 13.3 %collective-permute-start.10 = (bf16[1,8,24,512]{3,1,2,0:T(8,128)(2,1)S(1)}, bf16[1,8,24,512]{3,1,2,0:T(8,128)(2,1)S(1)}, u32[]{:S(2)}, u32[]{:S(2)}) collective-permute-start(bf16[1,8,24,512]{3,1,2,0:T(8,128)(2,1)S(1)} %slice_bitcast_fusion.1), channel_id=1, source_target_pairs={{8,0},{16,8},{24,16},{9,1},{17,9},{25,17},{10,2},{18,10},{26,18},{... | collective-permute-start | bytes 589832 | tf_op jit(solution)/shard_map/ppermute | solution.py:17
  658.1 22.4 %copy-start.114 = (bf16[1,8,24,512]{3,2,1,0:T(8,128)(2,1)S(1)}, bf16[1,8,24,512]{3,2,1,0:T(8,128)(2,1)}, u32[]{:S(2)}) copy-start(bf16[1,8,24,512]{3,2,1,0:T(8,128)(2,1)} %get-tuple-element.237) | copy-start | bytes 589828
  679.2 13.4 %collective-permute-start.11 = (bf16[1,8,24,512]{3,1,2,0:T(8,128)(2,1)S(1)}, bf16[1,8,24,512]{3,1,2,0:T(8,128)(2,1)S(1)}, u32[]{:S(2)}, u32[]{:S(2)}) collective-permute-start(bf16[1,8,24,512]{3,1,2,0:T(8,128)(2,1)S(1)} %slice_bitcast_fusion), channel_id=1, source_target_pairs={{8,0},{16,8},{24,16},{9,1},{17,9},{25,17},{10,2},{18,10},{26,18},{... | collective-permute-start | bytes 589832 | tf_op jit(solution)/shard_map/ppermute | solution.py:17
  696.5 30.0 %copy-start.113 = (bf16[1,8,24,512]{3,2,1,0:T(8,128)(2,1)S(1)}, bf16[1,8,24,512]{3,2,1,0:T(8,128)(2,1)}, u32[]{:S(2)}) copy-start(bf16[1,8,24,512]{3,2,1,0:T(8,128)(2,1)} %get-tuple-element.236) | copy-start | bytes 589828
  699.5 28.3 %copy-start.74 = (bf16[1,1,8,24,512]{4,2,3,1,0:T(8,128)(2,1)S(1)}, bf16[1,1,8,24,512]{4,2,3,1,0:T(8,128)(2,1)}, u32[]{:S(2)}) copy-start(bf16[1,1,8,24,512]{4,2,3,1,0:T(8,128)(2,1)} %get-tuple-element.130) | copy-start | bytes 589828
  762.4 20.9 %copy-start.55 = (bf16[8,8,4,512]{3,1,2,0:T(8,128)(2,1)S(1)}, bf16[8,8,4,512]{3,1,2,0:T(8,128)(2,1)}, u32[]{:S(2)}) copy-start(bf16[8,8,4,512]{3,1,2,0:T(8,128)(2,1)} %copy-done.54) | copy-start | bytes 786436
  762.4 23.0 %copy-start.101 = (f32[1,1,8,24]{2,3,1,0:T(8,128)S(1)}, f32[1,1,8,24]{2,3,1,0:T(8,128)}, u32[]{:S(2)}) copy-start(f32[1,1,8,24]{2,3,1,0:T(8,128)} %get-tuple-element.155) | copy-start | bytes 2308
  762.4 23.1 %copy-start.130 = (f32[1,512]{1,0:T(1,128)S(1)}, f32[1,512]{1,0:T(1,128)}, u32[]{:S(2)}) copy-start(f32[1,512]{1,0:T(1,128)} %get-tuple-element.165) | copy-start | bytes 6148
  762.6 22.9 %copy-start.131 = (f32[1,512]{1,0:T(1,128)S(1)}, f32[1,512]{1,0:T(1,128)}, u32[]{:S(2)}) copy-start(f32[1,512]{1,0:T(1,128)} %get-tuple-element.234) | copy-start | bytes 6148
  770.2 23.1 %all-to-all-start = ((bf16[4,1,8,24,512]{4,2,3,1,0:T(8,128)(2,1)}), bf16[4,1,8,24,512]{4,2,3,1,0:T(8,128)(2,1)S(1)}, u32[]{:S(2)}, u32[]{:S(2)}) async-start(bf16[4,1,8,24,512]{4,2,3,1,0:T(8,128)(2,1)} %pad_maximum_fusion), calls=%async_computation | async-start | bytes 1572864 | tf_op jit(solution)/shard_map/all_to_all | solution.py:203
  793.2 13.9 %all-to-all-start.1 = ((bf16[4,1,8,24,512]{4,2,3,1,0:T(8,128)(2,1)}), bf16[4,1,8,24,512]{4,2,3,1,0:T(8,128)(2,1)S(1)}, u32[]{:S(2)}, u32[]{:S(2)}) async-start(bf16[4,1,8,24,512]{4,2,3,1,0:T(8,128)(2,1)} %pad_maximum_fusion.1), calls=%async_computation.1 | async-start | bytes 1572864 | tf_op jit(solution)/shard_map/all_to_all | solution.py:204
  (127 other events, 827.8 us)
Sparse Core Ops, SparseCore 0:
  761.5 105.8 reduce-scatter.1
where the time goes:
time: 888 us; the launch traced here: 875 us
  blocking collectives  205 us (23%)
  local copies, waits for them, and re-layouts  197 us (22%)
  other arithmetic  182 us (20%)
  matrix products  142 us (16%)
  waiting for transfers between devices  79.5 us (9%)
  starting transfers between devices  50.2 us (6%)
  between operations  18.3 us (2%)
    psum x7, blocking collectives, layer_forward(): lax.psum((jnp.sum(pre_norm * inside, axis=(0, 1, 2)), jnp.sum(pre_norm *...  107 us
    psum x7, blocking collectives, layer_backward(): lax.psum((jnp.sum(grad_act, axis=(0, 1, 2)), jnp.sum(grad_act * normed, a...  98.9 us
    dot_general x63, matrix products, weight_back(): jnp.einsum('nhwi,nhwo->io', window, grad_pre, preferred_element_type=jnp....  89.8 us
    reduce_scatter x1, waiting for transfers between devices, shards(): lax.psum_scatter(weight_sum[None], 'dp', scatter_dimension=1, tiled=True)  59.6 us
    ppermute x12, starting transfers between devices, from_behind(): return lax.ppermute(x, axis, pairs)  34.4 us
    div x29, local copies, waits for them, and re-layouts, window_pool(): weights = raised / jnp.sum(raised, axis=(2, 4), keepdims=True)  30.5 us
    sub x29, local copies, waits for them, and re-layouts, window_pool(): raised = jnp.exp(blocks - window_max)  29.1 us
    add x1, other arithmetic, shards(): weight_sum = weight_sum + valid * weight_term  26.8 us
  transfers between devices with their start and end apart: 15, of which 8 were waited for; matrix products, arithmetic and copies ran while one was open for 17% of the time, Pallas kernels for 0%

commit v1 on v0

--- a/solution.py
+++ b/solution.py
@@ -3,6 +3,8 @@
 import jax
 import jax.numpy as jnp
 from jax import lax
+from jax.experimental import pallas as pl
+from jax.experimental.pallas import tpu as pltpu
 from jax.sharding import PartitionSpec as P
 
 CONVS = 2
@@ -127,7 +129,7 @@
     return (grad_in, weight_term, sums[1], sums[0])
 
 
-def shards(images, image_group, group_size, conv_weight, bn_gain, bn_bias, cotangent):
+def pipeline_shards(images, image_group, group_size, conv_weight, bn_gain, bn_bias, cotangent):
     section_index = lax.axis_index("section")
     sections = lax.axis_size("section")
     micro_total = images.shape[0]
@@ -212,6 +214,557 @@
     return (activations, input_grad, weight_grad, gain_grad, bias_grad)
 
 
+AXES = ("section", "dp")
+TAPS = 9
+VMEM_LIMIT = 40 * 1024 * 1024
+META_ROWS = 16
+
+
+def place():
+    dp_index = lax.axis_index("dp")
+    return lax.axis_index("section"), dp_index // 2, dp_index % 2
+
+
+def peer_order():
+    return [(k, j) for j in range(2) for k in range(4)]
+
+
+def slice_at(section, core, k, j):
+    return (section ^ k) * 2 + (core ^ j)
+
+
+def send(x, target):
+    sections = lax.axis_size("section")
+    dps = lax.axis_size("dp")
+    pairs = []
+    for s in range(sections):
+        for d in range(dps):
+            ts, tz, tc = target(s, d // 2, d % 2)
+            pairs.append((s * dps + d, ts * dps + tz * 2 + tc))
+    return lax.ppermute(x, AXES, pairs)
+
+
+def to_section(x, k):
+    return send(x, lambda s, z, c: (s ^ k, z, c))
+
+
+def to_plane(x, k):
+    return send(x, lambda s, z, c: (s, z ^ k, c))
+
+
+def to_core(x):
+    return send(x, lambda s, z, c: (s, z, c ^ 1))
+
+
+def plane_gather(block):
+    own = [block] + [to_section(block, k) for k in (1, 2, 3)]
+    return own + [to_core(x) for x in own]
+
+
+def grid_facts(frames, rows, cols):
+    at = jnp.arange(frames * rows * cols, dtype=jnp.int32)
+    col = at % cols
+    row = (at // cols) % rows
+    facts = [row > 0, row < rows - 1, col > 0, col < cols - 1, col % 2 == 0, row % 2 == 0]
+    facts = facts + [row < 0, row < 0]
+    return jnp.stack(facts).astype(jnp.float32)
+
+
+def shift(x, by, axis=1):
+    length = x.shape[axis]
+    return pltpu.roll(x, (-by) % length, axis) if by % length else x
+
+
+def row_ok(facts, d):
+    return facts[0:1, :] if d < 0 else facts[1:2, :]
+
+
+def col_ok(facts, d):
+    return facts[2:3, :] if d < 0 else facts[3:4, :]
+
+
+def sum_taps(taps_ref, facts, cols, sign):
+    ch = taps_ref.shape[0] // TAPS
+    total = None
+    for dx in (-1, 0, 1):
+        column = None
+        for dy in (-1, 0, 1):
+            tap = (dy + 1) * 3 + dx + 1
+            piece = taps_ref[tap * ch : (tap + 1) * ch, :]
+            if dy:
+                piece = shift(piece, sign * dy * cols) * row_ok(facts, sign * dy)
+            column = piece if column is None else column + piece
+        if dx:
+            column = shift(column, sign * dx) * col_ok(facts, sign * dx)
+        total = column if total is None else total + column
+    return total
+
+
+def window_op(x, op, facts, cols):
+    even_col = facts[4:5, :] > 0.5
+    even_row = facts[5:6, :] > 0.5
+    x = op(x, jnp.where(even_col, shift(x, 1), shift(x, -1)))
+    return op(x, jnp.where(even_row, shift(x, cols), shift(x, -cols)))
+
+
+def soft_pool(hidden, facts, cols):
+    raised = jnp.exp(hidden - window_op(hidden, jnp.maximum, facts, cols))
+    weights = raised / window_op(raised, jnp.add, facts, cols)
+    return weights, window_op(weights * hidden, jnp.add, facts, cols)
+
+
+def lane_sum(x):
+    return jnp.sum(x, axis=1, keepdims=True)
+
+
+def normalise(pre, inside):
+    count = lane_sum(inside)
+    mean = lane_sum(pre * inside) / count
+    square = lane_sum(pre * pre * inside) / count
+    scale = lax.rsqrt(square - mean * mean + eps)
+    return (pre - mean) * scale, scale
+
+
+def hidden_of(normed, gain, bias, inside, facts, cols, pooling):
+    pre_act = normed * gain + bias
+    hidden = pre_act * jax.nn.sigmoid(pre_act) * inside
+    if pooling:
+        weights, pooled = soft_pool(hidden, facts, cols)
+        hidden = weights * pooled * inside
+    return hidden
+
+
+def norm_back(grad, normed, scale, gain, bias, inside, facts, cols, pooling):
+    pre_act = normed * gain + bias
+    gate = jax.nn.sigmoid(pre_act)
+    if pooling:
+        hidden = pre_act * gate * inside
+        weights, pooled = soft_pool(hidden, facts, cols)
+        out = grad * inside
+        d_pooled = window_op(weights * out, jnp.add, facts, cols)
+        d_weights = out * pooled + d_pooled * hidden
+        spread = window_op(weights * d_weights, jnp.add, facts, cols)
+        grad = weights * (d_pooled + d_weights - spread)
+    grad_act = grad * inside * gate * (1.0 + pre_act * (1.0 - gate))
+    count = lane_sum(inside)
+    shift_sum = lane_sum(grad_act)
+    slope_sum = lane_sum(grad_act * normed)
+    grad_pre = inside * (scale * gain) * (grad_act - shift_sum / count - normed * (slope_sum / count))
+    return grad_pre.astype(jnp.bfloat16), shift_sum, slope_sum
+
+
+def assemble(blocks, full_ref):
+    section, _, core = place()
+    ch = blocks[0].shape[0]
+    for (k, j), block in zip(peer_order(), blocks):
+        at = pl.multiple_of(slice_at(section, core, k, j) * ch, ch)
+        full_ref[pl.ds(at, ch), :] = block[...]
+
+
+def assemble_frames(blocks, full_ref, cells):
+    _, plane, core = place()
+    for (k, j), block in zip(peer_order(), blocks):
+        frame = (plane ^ k) * 2 + (core ^ j)
+        full_ref[pl.ds(pl.multiple_of(frame * cells, cells), cells), :] = block[:cells, :]
+
+
+def tap_products(weight_ref, full_ref, taps_ref, transposed):
+    length = taps_ref.shape[1]
+    step = 512 if length % 512 == 0 else length
+    for at in range(0, length, step):
+        if transposed:
+            taps_ref[:, at : at + step] = lax.dot_general(
+                weight_ref[...],
+                full_ref[at : at + step, :],
+                (((1,), (1,)), ((), ())),
+                preferred_element_type=jnp.float32,
+            )
+        else:
+            taps_ref[:, at : at + step] = jnp.dot(
+                weight_ref[...], full_ref[:, at : at + step], preferred_element_type=jnp.float32
+            )
+
+
+def forward_kernel(dims, first, pooling, *refs):
+    blocks, (weight, gain, bias, inside, facts), (hidden, normed, scale), (full, taps) = (
+        refs[:8],
+        refs[8:13],
+        refs[13:16],
+        refs[16:],
+    )
+    rows, cols = dims
+    if first:
+        assemble_frames(blocks, full, rows * cols)
+    else:
+        assemble(blocks, full)
+    tap_products(weight, full, taps, first)
+    facts_now, inside_now = facts[...], inside[...]
+    pre = sum_taps(taps, facts_now, cols, 1)
+    normed_now, scale_now = normalise(pre, inside_now)
+    normed[...] = normed_now
+    scale[...] = scale_now
+    hidden[...] = hidden_of(
+        normed_now, gain[...], bias[...], inside_now, facts_now, cols, pooling
+    ).astype(jnp.bfloat16)
+
+
+def turn_kernel(dims, pooling, *refs):
+    blocks, cots = refs[:8], refs[8:16]
+    weight, gain, bias, inside, facts, pick = refs[16:22]
+    pieces, (grad_pre, shift_sum, slope_sum), (full, taps, cot_full, hidden) = (
+        refs[22:26],
+        refs[26:29],
+        refs[29:],
+    )
+    rows, cols = dims
+    assemble(blocks, full)
+    assemble_frames(cots, cot_full, rows * cols)
+    tap_products(weight, full, taps, False)
+    facts_now, inside_now = facts[...], inside[...]
+    pre = sum_taps(taps, facts_now, cols, 1)
+    normed, scale = normalise(pre, inside_now)
+    hidden[...] = hidden_of(
+        normed, gain[...], bias[...], inside_now, facts_now, cols, pooling
+    ).astype(jnp.bfloat16)
+    cut_frames(hidden, pieces)
+    cotangent = lax.dot_general(
+        pick[...], cot_full[...], (((1,), (1,)), ((), ())), preferred_element_type=jnp.float32
+    )
+    grad_pre[...], shift_sum[...], slope_sum[...] = norm_back(
+        cotangent, normed, scale, gain[...], bias[...], inside_now, facts_now, cols, pooling
+    )
+
+
+def cut_frames(full, pieces):
+    section, _, _ = place()
+    width = pieces[0].shape[1]
+    for k, piece in enumerate(pieces):
+        piece[...] = full[:, pl.ds(pl.multiple_of((section ^ k) * width, width), width)]
+
+
+def back_kernel(dims, pooling, *refs):
+    blocks, (weight, normed, scale, gain, bias, inside, facts) = refs[:8], refs[8:15]
+    (grad_pre, shift_sum, slope_sum), (full, taps) = refs[15:18], refs[18:]
+    assemble(blocks, full)
+    tap_products(weight, full, taps, False)
+    facts_now, inside_now = facts[...], inside[...]
+    grad = sum_taps(taps, facts_now, dims[1], -1).astype(jnp.bfloat16).astype(jnp.float32)
+    grad_pre[...], shift_sum[...], slope_sum[...] = norm_back(
+        grad, normed[...], scale[...], gain[...], bias[...], inside_now, facts_now, dims[1], pooling
+    )
+
+
+def input_kernel(dims, *refs):
+    blocks, (weight, inside, facts), pieces, (full, taps, grad) = (
+        refs[:8],
+        refs[8:11],
+        refs[11:15],
+        refs[15:],
+    )
+    assemble(blocks, full)
+    tap_products(weight, full, taps, False)
+    grad[...] = (sum_taps(taps, facts[...], dims[1], -1) * inside[...]).astype(jnp.bfloat16)
+    cut_frames(grad, pieces)
+
+
+def weight_kernel(dims, first, *refs):
+    blocks, (grad_pre, shift_sum, slope_sum, facts), pieces, (full, moved, product) = (
+        refs[:8],
+        refs[8:12],
+        refs[12:16],
+        refs[16:],
+    )
+    rows, cols = dims
+    _, plane, _ = place()
+    if first:
+        assemble_frames(blocks, full, rows * cols)
+    else:
+        assemble(blocks, full)
+    facts_now = facts[...]
+    grad = grad_pre[...].astype(jnp.float32)
+    ch = grad.shape[0]
+    for dx in (-1, 0, 1):
+        column = shift(grad, -dx) * col_ok(facts_now, -dx) if dx else grad
+        for dy in (-1, 0, 1):
+            piece = shift(column, -dy * cols) * row_ok(facts_now, -dy) if dy else column
+            tap = (dy + 1) * 3 + dx + 1
+            moved[tap * ch : (tap + 1) * ch, :] = piece.astype(jnp.bfloat16)
+    if first:
+        value = jnp.dot(moved[...], full[...], preferred_element_type=jnp.float32)
+    else:
+        value = lax.dot_general(
+            moved[...], full[...], (((1,), (1,)), ((), ())), preferred_element_type=jnp.float32
+        )
+    product[...] = value.astype(jnp.bfloat16)
+    width = pieces[0].shape[1]
+    lines = []
+    for sums in (shift_sum, slope_sum):
+        turned = jnp.broadcast_to(sums[...], (ch, width)).T
+        lines.append(jnp.concatenate([turned, jnp.zeros((width, width - ch), jnp.float32)], axis=1)[0:1])
+    sums_block = jnp.concatenate(lines + [jnp.zeros((META_ROWS - 2, width), jnp.float32)], axis=0)
+    for k, piece in enumerate(pieces):
+        piece[: TAPS * ch, :] = product[:, pl.ds(pl.multiple_of((plane ^ k) * width, width), width)]
+        piece[TAPS * ch :, :] = sums_block.astype(jnp.bfloat16)
+
+
+def pack_kernel(picks, weight, *outs):
+    turned = lax.dot_general(
+        picks[...], weight[0], (((1,), (1,)), ((), ())), preferred_element_type=jnp.float32
+    ).astype(jnp.bfloat16)
+    ch = outs[0].shape[1]
+    for k, out in enumerate(outs):
+        out[0] = turned[k * ch : (k + 1) * ch, :]
+
+
+def map_out_kernel(*refs):
+    blocks, out, full = refs[:8], refs[8], refs[9:]
+    section_plane, core = place()[1], place()[2]
+    (full,) = full
+    ch = blocks[0].shape[0]
+    for (k, j), block in zip(peer_order(), blocks):
+        at = pl.multiple_of(slice_at(section_plane, core, k, j) * ch, ch)
+        full[pl.ds(at, ch), :] = block[...]
+    cells = out.shape[0]
+    both = full[...].astype(jnp.float32)
+    mine = jnp.where(core == 0, both[:, :cells], both[:, cells:])
+    out[...] = mine.T.astype(out.dtype)
+
+
+def grads_out_kernel(*refs):
+    blocks, (weight_out, shift_out, slope_out), (full, turned) = refs[:8], refs[8:11], refs[11:]
+    section, plane, core = place()
+    taps, rows, channels = weight_out.shape
+    for tap in range(taps):
+        for (k, j), block in zip(peer_order(), blocks):
+            at = pl.multiple_of(slice_at(section, core, k, j) * rows, rows)
+            full[pl.ds(at, rows), :] = block[tap * rows : (tap + 1) * rows, :].astype(jnp.float32)
+        turned[...] = full[...].T
+        weight_out[tap] = turned[pl.ds(pl.multiple_of(core * rows, rows), rows), :]
+    shift_row = jnp.zeros((1, rows), jnp.float32)
+    slope_row = jnp.zeros((1, rows), jnp.float32)
+    for (k, j), block in zip(peer_order(), blocks):
+        if j == 0:
+            tail = block[taps * rows :, :].astype(jnp.float32)
+            mine = (section ^ k) == plane
+            shift_row = shift_row + jnp.where(mine, tail[0:1, :rows], 0.0)
+            slope_row = slope_row + jnp.where(mine, tail[1:2, :rows], 0.0)
+    shift_out[...] = shift_row
+    slope_out[...] = slope_row
+
+
+def call(kernel, outs, scratch, args, flops=0, name=None):
+    shapes = [jax.ShapeDtypeStruct(shape, dtype) for shape, dtype in outs]
+    moved = sum(a.size * a.dtype.itemsize for a in args)
+    moved += sum(s.size * s.dtype.itemsize for s in shapes)
+    return pl.pallas_call(
+        kernel,
+        out_shape=shapes,
+        in_specs=[pl.BlockSpec(memory_space=pltpu.VMEM)] * len(args),
+        out_specs=[pl.BlockSpec(memory_space=pltpu.VMEM)] * len(shapes),
+        scratch_shapes=[pltpu.VMEM(shape, dtype) for shape, dtype in scratch],
+        compiler_params=pltpu.CompilerParams(vmem_limit_bytes=VMEM_LIMIT),
+        cost_estimate=pl.CostEstimate(flops=flops, bytes_accessed=moved, transcendentals=0),
+        name=name,
+    )(*args)
+
+
+def one_hot(index, size):
+    return (index[:, None] == jnp.arange(size, dtype=jnp.int32)[None, :]).astype(jnp.bfloat16)
+
+
+def plane_shards(images, image_group, group_size, conv_weight, bn_gain, bn_bias, cotangent):
+    section, plane, core = place()
+    micro_total, _, rows, cols, channels = images.shape
+    layers = lax.axis_size("section")
+    cells = rows * cols
+    frames = 2 * micro_total
+    length = frames * cells
+    ch = channels // 8
+    dims = (rows, cols)
+    bf16, f32 = jnp.bfloat16, jnp.float32
+    facts = grid_facts(frames, rows, cols)
+    conv_flops = 2 * TAPS * ch * channels * length
+
+    taps_first = conv_weight[0].transpose(1, 2, 0, 3).reshape(TAPS, channels, channels)
+    row_at = jnp.arange(ch, dtype=jnp.int32)
+    picks = one_hot(
+        jnp.concatenate([slice_at(section, core, k, 0) * ch + row_at for k in range(4)]), channels
+    )
+    packed = pl.pallas_call(
+        pack_kernel,
+        grid=(TAPS,),
+        out_shape=[jax.ShapeDtypeStruct((TAPS, ch, channels), bf16)] * 4,
+        in_specs=[
+            pl.BlockSpec((4 * ch, channels), lambda t: (0, 0)),
+            pl.BlockSpec((1, channels, channels), lambda t: (t, 0, 0)),
+        ],
+        out_specs=[pl.BlockSpec((1, ch, channels), lambda t: (t, 0, 0))] * 4,
+        compiler_params=pltpu.CompilerParams(vmem_limit_bytes=VMEM_LIMIT),
+        name="weight_pack",
+    )(picks, taps_first)
+    packed = [x.reshape(TAPS * ch, channels) for x in packed]
+    out_rel = [packed[0]] + [to_section(packed[k], k) for k in (1, 2, 3)]
+
+    def of_layer(relative, layer):
+        return lax.select_n(section ^ layer, *relative)
+
+    inside_all = canvas_mask(image_group[:, 0], group_size, rows, cols)
+    masked = (images[:, 0].astype(f32) * inside_all).astype(bf16).reshape(micro_total, cells, channels)
+    meta = jnp.broadcast_to(
+        image_group[:, :, None].astype(bf16), (micro_total, META_ROWS, channels)
+    )
+    payload = jnp.concatenate([masked, meta], axis=1)
+    mine = [lax.dynamic_index_in_dim(payload, plane ^ k, 0, keepdims=False) for k in range(4)]
+    frames_in = [mine[0]] + [to_plane(mine[k], k) for k in (1, 2, 3)]
+    frames_in = frames_in + [to_core(x) for x in frames_in]
+    at = jnp.stack([(plane ^ k) * 2 + (core ^ j) for k, j in peer_order()])
+    groups = jnp.stack([x[cells, 0] for x in frames_in]).astype(jnp.int32)
+    ordered = jnp.sum(
+        jnp.where(at[None, :] == jnp.arange(frames, dtype=jnp.int32)[:, None], groups[None, :], 0), axis=1
+    )
+    inside = canvas_mask(ordered, group_size, rows, cols).reshape(1, length)
+
+    cot = lax.dynamic_slice_in_dim(
+        cotangent.reshape(micro_total, cells, channels), section * 2 * ch, 2 * ch, 2
+    )
+    mine = [lax.dynamic_index_in_dim(cot, plane ^ k, 0, keepdims=False) for k in range(4)]
+    cots = [mine[0]] + [to_plane(mine[k], k) for k in (1, 2, 3)]
+    cots = cots + [to_core(x) for x in cots]
+    half = one_hot(core * ch + row_at, 2 * ch)
+
+    both = jnp.stack([bn_gain[0].reshape(8, ch), bn_bias[0].reshape(8, ch)], axis=1)
+    rel = [both[slice_at(section, core, k, 0)] for k in range(4)]
+    rel = [rel[0]] + [to_section(rel[k], k) for k in (1, 2, 3)]
+    gains, biases = [], []
+    for layer in range(layers):
+        pair = lax.select_n(section ^ layer, *rel)
+        gains.append(pair[0][:, None])
+        biases.append(pair[1][:, None])
+
+    full_map = ((channels, length), bf16)
+    full_frames = ((length, channels), bf16)
+    tap_scratch = ((TAPS * ch, length), f32)
+    map_out = ((ch, length), bf16)
+    column = ((ch, 1), f32)
+    piece = ((ch, 2 * cells), bf16)
+
+    gathered = [frames_in]
+    kept = []
+    for layer in range(layers - 1):
+        hidden, normed, scale = call(
+            partial(forward_kernel, dims, layer == 0, layer == CONVS - 1),
+            [map_out, ((ch, length), f32), column],
+            [full_frames if layer == 0 else full_map, tap_scratch],
+            [*gathered[layer], of_layer(out_rel, layer), gains[layer], biases[layer], inside, facts],
+            conv_flops,
+            "forward",
+        )
+        kept.append((normed, scale))
+        gathered.append(plane_gather(hidden))
+    last = layers - 1
+    *pieces, grad_pre, shift_sum, slope_sum = call(
+        partial(turn_kernel, dims, last == CONVS - 1),
+        [piece] * 4 + [map_out, column, column],
+        [full_map, tap_scratch, ((length, 2 * ch), bf16), map_out],
+        [*gathered[last], *cots, of_layer(out_rel, last), gains[last], biases[last], inside, facts, half],
+        conv_flops,
+        "turn",
+    )
+
+    def deliver(pieces):
+        blocks = [send(x, lambda s, z, c, k=k: (z, s ^ k, c)) for k, x in enumerate(pieces)]
+        blocks = blocks + [to_core(x) for x in blocks]
+        (out,) = call(
+            map_out_kernel, [((cells, channels), bf16)], [((channels, 2 * cells), bf16)], blocks, 0, "map_out"
+        )
+        return out.reshape(1, 1, rows, cols, channels)
+
+    activations = deliver(pieces)
+
+    in_slices = taps_first.reshape(TAPS, 8, ch, channels)
+    in_own = [
+        lax.dynamic_index_in_dim(in_slices, slice_at(section, core, k, 0), 1, keepdims=False).reshape(
+            TAPS * ch, channels
+        )
+        for k in range(4)
+    ]
+    in_rel = [in_own[0]] + [to_section(in_own[k], k) for k in (1, 2, 3)]
+
+    def weight_share(layer, grad_pre, shift_sum, slope_sum):
+        first = layer == 0
+        parts = call(
+            partial(weight_kernel, dims, first),
+            [((TAPS * ch + META_ROWS, 2 * ch), bf16)] * 4,
+            [full_frames if first else full_map, ((TAPS * ch, length), bf16), ((TAPS * ch, channels), bf16)],
+            [*gathered[layer], grad_pre, shift_sum, slope_sum, facts],
+            conv_flops,
+            "weight_share",
+        )
+        parts = [parts[0]] + [to_plane(parts[k], k) for k in (1, 2, 3)]
+        return sum(x.astype(f32) for x in parts).astype(bf16)
+
+    shares = [None] * layers
+    for layer in range(last, -1, -1):
+        blocks = plane_gather(grad_pre)
+        shares[layer] = weight_share(layer, grad_pre, shift_sum, slope_sum)
+        if layer:
+            grad_pre, shift_sum, slope_sum = call(
+                partial(back_kernel, dims, layer - 1 == CONVS - 1),
+                [map_out, column, column],
+                [full_map, tap_scratch],
+                [
+                    *blocks,
+                    of_layer(in_rel, layer),
+                    *kept[layer - 1],
+                    gains[layer - 1],
+                    biases[layer - 1],
+                    inside,
+                    facts,
+                ],
+                conv_flops,
+                "back",
+            )
+        else:
+            pieces = call(
+                partial(input_kernel, dims),
+                [piece] * 4,
+                [full_map, tap_scratch, map_out],
+                [*blocks, of_layer(in_rel, 0), inside, facts],
+                conv_flops,
+                "input",
+            )
+    input_grad = deliver(pieces)
+
+    chosen = [lax.select_n(section ^ k, *shares) for k in range(4)]
+    blocks = [chosen[0]] + [to_section(chosen[k], k) for k in (1, 2, 3)]
+    blocks = blocks + [to_core(x) for x in blocks]
+    weight_grad, bias_grad, gain_grad = call(
+        grads_out_kernel,
+        [((TAPS, ch, channels), f32), ((1, ch), f32), ((1, ch), f32)],
+        [((channels, 2 * ch), f32), ((2 * ch, channels), f32)],
+        blocks,
+        0,
+        "grads_out",
+    )
+    weight_grad = weight_grad.reshape(3, 3, ch, channels).transpose(2, 0, 1, 3)[None]
+    return (activations, input_grad, weight_grad, gain_grad, bias_grad)
+
+
+def fits_plane_plan(images, conv_weight, sections, dps):
+    micro_total, images_total, rows, cols, channels = images.shape
+    return (
+        sections == 4
+        and dps == 2 * sections
+        and micro_total == sections
+        and conv_weight.shape[0] == sections
+        and images_total == dps
+        and rows % 2 == 0
+        and cols % 2 == 0
+        and (rows * cols) % 64 == 0
+        and channels == 512
+    )
+
+
 def solution(mesh):
     in_specs = (
         P(None, "dp", None, None, None),
@@ -229,4 +782,11 @@
         P("section", "dp"),
         P("section", "dp"),
     )
-    return jax.shard_map(shards, mesh=mesh, in_specs=in_specs, out_specs=out_specs, check_vma=False)
+    sections, dps = mesh.shape["section"], mesh.shape["dp"]
+
+    def program(images, image_group, group_size, conv_weight, bn_gain, bn_bias, cotangent):
+        plan = plane_shards if fits_plane_plan(images, conv_weight, sections, dps) else pipeline_shards
+        sharded = jax.shard_map(plan, mesh=mesh, in_specs=in_specs, out_specs=out_specs, check_vma=False)
+        return sharded(images, image_group, group_size, conv_weight, bn_gain, bn_bias, cotangent)
+
+    return program

time: 888 us -> 338 us (0.38); the launches traced: 875 us -> 336 us
  blocking collectives: 205 us -> 0 us
  other arithmetic: 182 us -> 11.6 us
  local copies, waits for them, and re-layouts: 197 us -> 28.7 us
  matrix products: 142 us -> 0 us
  waiting for transfers between devices: 79.5 us -> 143 us
  starting transfers between devices: 50.2 us -> 109 us
  Pallas kernels: 0 us -> 42.9 us
  between operations: 18.3 us -> 1.25 us
    psum x14 -> x0, blocking collectives: 205 us -> none  [the longest x7 107 us: layer_forward(): lax.psum((jnp.sum(pre_norm * inside, axis=(0, 1, 2)), jnp.sum(pre_norm *...]
    ppermute x12 -> x107, waiting for transfers between devices: 11.4 us -> 143 us  [send(): return lax.ppermute(x, AXES, pairs)]
    dot_general x63 -> x0, matrix products: 89.8 us -> none  [weight_back(): jnp.einsum('nhwi,nhwo->io', window, grad_pre, preferred_element_type=jnp....]
    ppermute x12 -> x107, starting transfers between devices: 34.4 us -> 109 us  [send(): return lax.ppermute(x, AXES, pairs)]
    reduce_sum x64 -> x1, other arithmetic: 73.2 us -> 0.12 us  [plane_shards(): jnp.sum(jnp.where(at[None, :] == jnp.arange(frames, dtype=jnp.int32)[:, N...]
    reduce_scatter x1 -> x0, waiting for transfers between devices: 59.6 us -> none  [shards(): lax.psum_scatter(weight_sum[None], 'dp', scatter_dimension=1, tiled=True)]
    conv_general_dilated x14 -> x0, matrix products: 52.5 us -> none  [the longest x7 26.4 us: conv_data_back(): lax.conv_general_dilated(grad_pre, flipped, (1, 1), 'SAME', dimension_num...]
    pallas_call x0 -> x16, Pallas kernels: none -> 42.9 us  [the longest x15 39.8 us: call(): pl.pallas_call(kernel, out_shape=shapes, in_specs=[pl.BlockSpec(memory_sp...]
  transfers between devices with their start and end apart: 15 -> 107, of which waited for: 8 -> 36; matrix products, arithmetic and copies ran while one was open for 17% -> 8% of each run, Pallas kernels for 0% -> 10%
where the time goes in v1:
time: 338 us; the launch traced here: 336 us
  waiting for transfers between devices  143 us (42%)
  starting transfers between devices  109 us (32%)
  Pallas kernels  42.9 us (13%)
  local copies, waits for them, and re-layouts  28.7 us (8%)
  other arithmetic  11.6 us (3%)
    ppermute x107, waiting for transfers between devices, send(): return lax.ppermute(x, AXES, pairs)  143 us
    ppermute x107, starting transfers between devices, send(): return lax.ppermute(x, AXES, pairs)  109 us
    pallas_call x15, Pallas kernels, call(): pl.pallas_call(kernel, out_shape=shapes, in_specs=[pl.BlockSpec(memory_sp...  39.8 us
    unnamed x43, local copies, waits for them, and re-layouts  9.89 us
    slice x8, local copies, waits for them, and re-layouts, plane_shards(): groups = jnp.stack([x[cells, 0] for x in frames_in]).astype(jnp.int32)  6.78 us
  transfers between devices with their start and end apart: 107, of which 36 were waited for; matrix products, arithmetic and copies ran while one was open for 8% of the time, Pallas kernels for 10%

profile of v1, /device:TPU:0, one launch (start us, length us, event | category | flops | bytes accessed | tf_op | source)
XLA Modules:
  0.0 335.8 jit_solution(6715790527711637875)
XLA Ops:
  4.0 4.0 %collective-permute-start.12 = (f32[2,64]{1,0:T(2,128)S(1)}, f32[2,64]{1,0:T(2,128)S(1)}, u32[]{:S(2)}, u32[]{:S(2)}) collective-permute-start(f32[2,64]{1,0:T(2,128)S(1)} %get-tuple-element.143), channel_id=1, source_target_pairs={{0,24},{1,25},{2,26},{3,27},{4,28},{5,29},{6,30},{7,31},{8,16},{9,... | collective-permute-start | bytes 1544 | tf_op jit(solution)/shard_map/ppermute | solution.py:244
  13.5 4.0 %collective-permute-start.2 = (bf16[208,512]{1,0:T(8,128)(2,1)}, bf16[208,512]{1,0:T(8,128)(2,1)S(1)}, u32[]{:S(2)}, u32[]{:S(2)}) collective-permute-start(bf16[208,512]{1,0:T(8,128)(2,1)} %get-tuple-element.132), channel_id=1, source_target_pairs={{0,6},{1,7},{2,4},{3,5},{4,2},{5,3},{6,0},{7,1},{8,14},{9,15},{10,... | collective-permute-start | bytes 638984 | tf_op jit(solution)/shard_map/ppermute | solution.py:244
  18.7 2.3 copy-done
  21.0 3.1 weight_pack.1
  24.8 1.7 collective-permute-start.7
  26.6 8.0 %collective-permute-done.refs_1_ = bf16[208,512]{1,0:T(8,128)(2,1)S(1)} collective-permute-done((bf16[208,512]{1,0:T(8,128)(2,1)}, bf16[208,512]{1,0:T(8,128)(2,1)S(1)}, u32[]{:S(2)}, u32[]{:S(2)}) %collective-permute-start) | collective-permute-done | bytes 213024 | tf_op jit(solution)/shard_map/ppermute | solution.py:244
  34.6 3.2 collective-permute-done.1.refs_2_
  48.6 5.1 %stack.78 = bf16[8]{0:T(256)(128)(2,1)S(1)} concatenate(bf16[1]{0:T(256)(128)(2,1)} %bitcast.31, bf16[1]{0:T(256)(128)(2,1)} %bitcast.32, bf16[1]{0:T(256)(128)(2,1)} %bitcast.33, bf16[1]{0:T(256)(128)(2,1)} %bitcast.34, bf16[1]{0:T(256)(128)(2,1)} %bitcast.35, bf16[1]{0:T(256)(128)(2,1)} %bitcast.36, bf16[1]{0:T(256)(128)(2,1)} %bitcast.37, bf16[1]{0:T(256)(128)(2,1)} %bitcast.38), dimensions={0} | concatenate | bytes 32 | tf_op jit(solution)/shard_map/stack | solution.py:621
  54.3 15.1 %collective-permute-done.8 = bf16[576,512]{1,0:T(8,128)(2,1)} collective-permute-done((bf16[576,512]{1,0:T(8,128)(2,1)S(1)}, bf16[576,512]{1,0:T(8,128)(2,1)}, u32[]{:S(2)}, u32[]{:S(2)}) %collective-permute-start.8) | collective-permute-done | bytes 589856 | tf_op jit(solution)/shard_map/ppermute | solution.py:244
  69.4 1.8 fusion.8
  71.2 3.0 forward.3
  75.5 2.4 collective-permute-start.15
  79.0 5.2 %collective-permute-done.15.refs_3_ = bf16[64,1536]{1,0:T(8,128)(2,1)S(1)} collective-permute-done((bf16[64,1536]{1,0:T(8,128)(2,1)S(1)}, bf16[64,1536]{1,0:T(8,128)(2,1)S(1)}, u32[]{:S(2)}, u32[]{:S(2)}) %collective-permute-start.15) | collective-permute-done | bytes 196640 | tf_op jit(solution)/shard_map/ppermute | solution.py:244
  84.3 3.0 collective-permute-done.14.refs_2_
  89.3 5.1 %forward.4 = (bf16[64,1536]{1,0:T(8,128)(2,1)}, f32[64,1536]{1,0:T(8,128)S(1)}, f32[64,1]{1,0:T(8,128)S(1)}) custom-call(bf16[64,1536]{1,0:T(8,128)(2,1)S(1)} %get-tuple-element.61.refs_0_, bf16[64,1536]{1,0:T(8,128)(2,1)} %collective-permute-done.13.refs_1_, bf16[64,1536]{1,0:T(8,128)(2,1)} %collective-permute-done.14.refs_2_, ...), custom_call_target="tpu_custom_call" | custom-call | flops 905969664 | bytes 2808576 | tf_op jit(solution)/shard_map/forward/pallas_call | solution.py:559
  95.8 1.7 collective-permute-start.22
  99.3 5.4 %collective-permute-done.22.refs_3_ = bf16[64,1536]{1,0:T(8,128)(2,1)S(1)} collective-permute-done((bf16[64,1536]{1,0:T(8,128)(2,1)}, bf16[64,1536]{1,0:T(8,128)(2,1)S(1)}, u32[]{:S(2)}, u32[]{:S(2)}) %collective-permute-start.22) | collective-permute-done | bytes 196640 | tf_op jit(solution)/shard_map/ppermute | solution.py:244
  104.7 3.5 %collective-permute-done.21.refs_2_ = bf16[64,1536]{1,0:T(8,128)(2,1)S(1)} collective-permute-done((bf16[64,1536]{1,0:T(8,128)(2,1)}, bf16[64,1536]{1,0:T(8,128)(2,1)S(1)}, u32[]{:S(2)}, u32[]{:S(2)}) %collective-permute-start.21) | collective-permute-done | bytes 196640 | tf_op jit(solution)/shard_map/ppermute | solution.py:244
  108.7 1.8 dynamic-slice_bitcast_fusion
  111.8 4.5 %collective-permute-done.36.refs_11_ = bf16[192,128]{1,0:T(8,128)(2,1)S(1)} collective-permute-done((bf16[192,128]{1,0:T(8,128)(2,1)S(1)}, bf16[192,128]{1,0:T(8,128)(2,1)S(1)}, u32[]{:S(2)}, u32[]{:S(2)}) %collective-permute-start.36) | collective-permute-done | bytes 49184 | tf_op jit(solution)/shard_map/ppermute | solution.py:244
  116.5 4.8 %collective-permute-done.35.refs_10_ = bf16[192,128]{1,0:T(8,128)(2,1)S(1)} collective-permute-done((bf16[192,128]{1,0:T(8,128)(2,1)S(1)}, bf16[192,128]{1,0:T(8,128)(2,1)S(1)}, u32[]{:S(2)}, u32[]{:S(2)}) %collective-permute-start.35) | collective-permute-done | bytes 49184 | tf_op jit(solution)/shard_map/ppermute | solution.py:244
  121.9 3.6 %forward.5 = (bf16[64,1536]{1,0:T(8,128)(2,1)}, f32[64,1536]{1,0:T(8,128)S(1)}, f32[64,1]{1,0:T(8,128)S(1)}) custom-call(bf16[64,1536]{1,0:T(8,128)(2,1)} %get-tuple-element.62.refs_0_, bf16[64,1536]{1,0:T(8,128)(2,1)S(1)} %collective-permute-done.20.refs_1_, bf16[64,1536]{1,0:T(8,128)(2,1)S(1)} %collective-permute-done.21.refs_2_, ...), custom_call_target="tpu_custom_call" | custom-call | flops 905969664 | bytes 2808576 | tf_op jit(solution)/shard_map/forward/pallas_call | solution.py:559
  127.4 1.6 collective-permute-start.29
  130.3 3.0 constant_dynamic-slice_fusion
  138.6 13.5 %collective-permute-done.28.refs_2_ = bf16[64,1536]{1,0:T(8,128)(2,1)} collective-permute-done((bf16[64,1536]{1,0:T(8,128)(2,1)}, bf16[64,1536]{1,0:T(8,128)(2,1)}, u32[]{:S(2)}, u32[]{:S(2)}) %collective-permute-start.28) | collective-permute-done | bytes 196640 | tf_op jit(solution)/shard_map/ppermute | solution.py:244
  152.2 16.5 %collective-permute-done.27.refs_1_ = bf16[64,1536]{1,0:T(8,128)(2,1)} collective-permute-done((bf16[64,1536]{1,0:T(8,128)(2,1)}, bf16[64,1536]{1,0:T(8,128)(2,1)}, u32[]{:S(2)}, u32[]{:S(2)}) %collective-permute-start.27) | collective-permute-done | bytes 196640 | tf_op jit(solution)/shard_map/ppermute | solution.py:244
  172.2 3.6 %turn.1 = (bf16[64,384]{1,0:T(8,128)(2,1)S(1)}, bf16[64,384]{1,0:T(8,128)(2,1)S(1)}, bf16[64,384]{1,0:T(8,128)(2,1)S(1)}, bf16[64,384]{1,0:T(8,128)(2,1)S(1)}, b...) custom-call(bf16[64,1536]{1,0:T(8,128)(2,1)} %get-tuple-element.63.refs_0_, ...), custom_call_target="tpu_custom_call" | custom-call | flops 905969664 | bytes 3021824 | tf_op jit(solution)/shard_map/turn/pallas_call | solution.py:559
  175.7 1.6 collective-permute-start.51
  179.3 5.2 %collective-permute-done.51.refs_3_ = bf16[64,1536]{1,0:T(8,128)(2,1)S(1)} collective-permute-done((bf16[64,1536]{1,0:T(8,128)(2,1)S(1)}, bf16[64,1536]{1,0:T(8,128)(2,1)S(1)}, u32[]{:S(2)}, u32[]{:S(2)}) %collective-permute-start.51) | collective-permute-done | bytes 196640 | tf_op jit(solution)/shard_map/ppermute | solution.py:244
  184.5 3.6 %collective-permute-done.50.refs_2_ = bf16[64,1536]{1,0:T(8,128)(2,1)S(1)} collective-permute-done((bf16[64,1536]{1,0:T(8,128)(2,1)S(1)}, bf16[64,1536]{1,0:T(8,128)(2,1)S(1)}, u32[]{:S(2)}, u32[]{:S(2)}) %collective-permute-start.50) | collective-permute-done | bytes 196640 | tf_op jit(solution)/shard_map/ppermute | solution.py:244
  188.6 1.8 fusion.4
  190.5 1.7 back.3
  192.2 1.6 collective-permute-start.61
  195.7 5.2 %collective-permute-done.61.refs_3_ = bf16[64,1536]{1,0:T(8,128)(2,1)S(1)} collective-permute-done((bf16[64,1536]{1,0:T(8,128)(2,1)S(1)}, bf16[64,1536]{1,0:T(8,128)(2,1)S(1)}, u32[]{:S(2)}, u32[]{:S(2)}) %collective-permute-start.61) | collective-permute-done | bytes 196640 | tf_op jit(solution)/shard_map/ppermute | solution.py:244
  200.9 3.2 collective-permute-done.60.refs_2_
  205.9 4.1 %back.4 = (bf16[64,1536]{1,0:T(8,128)(2,1)S(1)}, f32[64,1]{1,0:T(8,128)S(1)}, f32[64,1]{1,0:T(8,128)S(1)}) custom-call(bf16[64,1536]{1,0:T(8,128)(2,1)S(1)} %get-tuple-element.71.refs_0_.refs_8_, bf16[64,1536]{1,0:T(8,128)(2,1)S(1)} %collective-permute-done.59.refs_1_, bf16[64,1536]{1,0:T(8,128)(2,1)S(1)} %collective-permute-done.60.refs_2_, ...), custom_call_target="tpu_custom_call" | custom-call | flops 905969664 | bytes 2809088 | tf_op jit(solution)/shard_map/back/pallas_call | solution.py:559
  210.0 4.7 %collective-permute-start.68 = (bf16[64,1536]{1,0:T(8,128)(2,1)S(1)}, bf16[64,1536]{1,0:T(8,128)(2,1)S(1)}, u32[]{:S(2)}, u32[]{:S(2)}) collective-permute-start(bf16[64,1536]{1,0:T(8,128)(2,1)S(1)} %get-tuple-element.74.refs_0_.refs_8_), channel_id=1, source_target_pairs={{0,24},{1,25},{2,26},{3,27},{4,28},{5,29},{6,30},{7,31},{8,16},{9,... | collective-permute-start | bytes 589832 | tf_op jit(solution)/shard_map/ppermute | solution.py:244
  215.8 2.9 weight_share.7
  220.8 5.3 %collective-permute-done.42.refs_1_ = bf16[64,384]{1,0:T(8,128)(2,1)S(1)} collective-permute-done((bf16[64,384]{1,0:T(8,128)(2,1)S(1)}, bf16[64,384]{1,0:T(8,128)(2,1)S(1)}, u32[]{:S(2)}, u32[]{:S(2)}) %collective-permute-start.42) | collective-permute-done | bytes 49184 | tf_op jit(solution)/shard_map/ppermute | solution.py:244
  226.1 3.3 collective-permute-start.43
  229.4 1.8 collective-permute-done.43.refs_2_
  232.2 3.2 collective-permute-start.98
  235.5 3.0 weight_share.6
  238.5 3.0 weight_share.5
  242.9 3.5 %collective-permute-start.99 = (bf16[592,128]{1,0:T(8,128)(2,1)S(1)}, bf16[592,128]{1,0:T(8,128)(2,1)S(1)}, u32[]{:S(2)}, u32[]{:S(2)}) collective-permute-start(bf16[592,128]{1,0:T(8,128)(2,1)S(1)} %get-tuple-element.105), channel_id=1, source_target_pairs={{0,6},{1,7},{2,4},{3,5},{4,2},{5,3},{6,0},{7,1},{8,14},{9,15},{10,... | collective-permute-start | bytes 454664 | tf_op jit(solution)/shard_map/ppermute | solution.py:244
  247.3 3.5 %collective-permute-start.96 = (bf16[592,128]{1,0:T(8,128)(2,1)S(1)}, bf16[592,128]{1,0:T(8,128)(2,1)S(1)}, u32[]{:S(2)}, u32[]{:S(2)}) collective-permute-start(bf16[592,128]{1,0:T(8,128)(2,1)S(1)} %get-tuple-element.99), channel_id=1, source_target_pairs={{0,6},{1,7},{2,4},{3,5},{4,2},{5,3},{6,0},{7,1},{8,14},{9,15},{10,... | collective-permute-start | bytes 454664 | tf_op jit(solution)/shard_map/ppermute | solution.py:244
  250.8 1.7 back.5
  252.6 2.9 weight_share.4
  256.4 3.9 %collective-permute-start.93 = (bf16[592,128]{1,0:T(8,128)(2,1)S(1)}, bf16[592,128]{1,0:T(8,128)(2,1)S(1)}, u32[]{:S(2)}, u32[]{:S(2)}) collective-permute-start(bf16[592,128]{1,0:T(8,128)(2,1)S(1)} %get-tuple-element.93), channel_id=1, source_target_pairs={{0,6},{1,7},{2,4},{3,5},{4,2},{5,3},{6,0},{7,1},{8,14},{9,15},{10,... | collective-permute-start | bytes 454664 | tf_op jit(solution)/shard_map/ppermute | solution.py:244
  260.2 2.9 collective-permute-done.95
  263.2 9.0 %collective-permute-start.89 = (bf16[592,128]{1,0:T(8,128)(2,1)S(1)}, bf16[592,128]{1,0:T(8,128)(2,1)S(1)}, u32[]{:S(2)}, u32[]{:S(2)}) collective-permute-start(bf16[592,128]{1,0:T(8,128)(2,1)S(1)} %get-tuple-element.86), channel_id=1, source_target_pairs={{0,4},{1,5},{2,6},{3,7},{4,0},{5,1},{6,2},{7,3},{8,12},{9,13},{10,... | collective-permute-start | bytes 454664 | tf_op jit(solution)/shard_map/ppermute | solution.py:244
  272.2 3.4 %collective-permute-start.90 = (bf16[592,128]{1,0:T(8,128)(2,1)S(1)}, bf16[592,128]{1,0:T(8,128)(2,1)S(1)}, u32[]{:S(2)}, u32[]{:S(2)}) collective-permute-start(bf16[592,128]{1,0:T(8,128)(2,1)S(1)} %get-tuple-element.87), channel_id=1, source_target_pairs={{0,6},{1,7},{2,4},{3,5},{4,2},{5,3},{6,0},{7,1},{8,14},{9,15},{10,... | collective-permute-start | bytes 454664 | tf_op jit(solution)/shard_map/ppermute | solution.py:244
  275.6 6.8 %collective-permute-done.92 = bf16[592,128]{1,0:T(8,128)(2,1)S(1)} collective-permute-done((bf16[592,128]{1,0:T(8,128)(2,1)S(1)}, bf16[592,128]{1,0:T(8,128)(2,1)S(1)}, u32[]{:S(2)}, u32[]{:S(2)}) %collective-permute-start.92) | collective-permute-done | bytes 151584 | tf_op jit(solution)/shard_map/ppermute | solution.py:244
  283.0 6.0 %collective-permute-done.89 = bf16[592,128]{1,0:T(8,128)(2,1)S(1)} collective-permute-done((bf16[592,128]{1,0:T(8,128)(2,1)S(1)}, bf16[592,128]{1,0:T(8,128)(2,1)S(1)}, u32[]{:S(2)}, u32[]{:S(2)}) %collective-permute-start.89) | collective-permute-done | bytes 151584 | tf_op jit(solution)/shard_map/ppermute | solution.py:244
  291.1 3.3 collective-permute-start.74
  294.4 1.5 collective-permute-start.73
  298.4 5.9 %collective-permute-done.74.refs_2_ = bf16[64,1536]{1,0:T(8,128)(2,1)S(1)} collective-permute-done((bf16[64,1536]{1,0:T(8,128)(2,1)S(1)}, bf16[64,1536]{1,0:T(8,128)(2,1)S(1)}, u32[]{:S(2)}, u32[]{:S(2)}) %collective-permute-start.74) | collective-permute-done | bytes 196640 | tf_op jit(solution)/shard_map/ppermute | solution.py:244
  305.8 2.7 collective-permute-start.100
  309.4 2.8 collective-permute-done.100.refs_1_
  315.4 4.3 %collective-permute-start.81 = (bf16[64,384]{1,0:T(8,128)(2,1)S(1)}, bf16[64,384]{1,0:T(8,128)(2,1)S(1)}, u32[]{:S(2)}, u32[]{:S(2)}) collective-permute-start(bf16[64,384]{1,0:T(8,128)(2,1)S(1)} %get-tuple-element.79), channel_id=1, source_target_pairs={{0,2},{1,3},{2,10},{3,11},{4,18},{5,19},{6,26},{7,27},{8,0},{9,1},... | collective-permute-start | bytes 147464 | tf_op jit(solution)/shard_map/ppermute | solution.py:244
  319.7 5.8 %collective-permute-start.82 = (bf16[64,384]{1,0:T(8,128)(2,1)S(1)}, bf16[64,384]{1,0:T(8,128)(2,1)S(1)}, u32[]{:S(2)}, u32[]{:S(2)}) collective-permute-start(bf16[64,384]{1,0:T(8,128)(2,1)S(1)} %get-tuple-element.80), channel_id=1, source_target_pairs={{0,4},{1,5},{2,12},{3,13},{4,20},{5,21},{6,28},{7,29},{8,6},{9,7},... | collective-permute-start | bytes 147464 | tf_op jit(solution)/shard_map/ppermute | solution.py:244
  325.5 3.4 %collective-permute-start.83 = (bf16[64,384]{1,0:T(8,128)(2,1)S(1)}, bf16[64,384]{1,0:T(8,128)(2,1)S(1)}, u32[]{:S(2)}, u32[]{:S(2)}) collective-permute-start(bf16[64,384]{1,0:T(8,128)(2,1)S(1)} %get-tuple-element.81), channel_id=1, source_target_pairs={{0,6},{1,7},{2,14},{3,15},{4,22},{5,23},{6,30},{7,31},{8,4},{9,5},... | collective-permute-start | bytes 147464 | tf_op jit(solution)/shard_map/ppermute | solution.py:244
  328.9 2.5 collective-permute-done.83.refs_3_
  333.0 1.8 grads_out.1
  (273 shorter events, 71.2 us)
Async XLA Ops:
  4.0 20.1 %collective-permute-start.12 = (f32[2,64]{1,0:T(2,128)S(1)}, f32[2,64]{1,0:T(2,128)S(1)}, u32[]{:S(2)}, u32[]{:S(2)}) collective-permute-start(f32[2,64]{1,0:T(2,128)S(1)} %get-tuple-element.143), channel_id=1, source_target_pairs={{0,24},{1,25},{2,26},{3,27},{4,28},{5,29},{6,30},{7,31},{8,16},{9,... | collective-permute-start | bytes 1544 | tf_op jit(solution)/shard_map/ppermute | solution.py:244
  8.0 16.3 %collective-permute-start.10 = (f32[2,64]{1,0:T(2,128)S(1)}, f32[2,64]{1,0:T(2,128)S(1)}, u32[]{:S(2)}, u32[]{:S(2)}) collective-permute-start(f32[2,64]{1,0:T(2,128)S(1)} %get-tuple-element.144), channel_id=1, source_target_pairs={{0,8},{1,9},{2,10},{3,11},{4,12},{5,13},{6,14},{7,15},{8,0},{9,1},... | collective-permute-start | bytes 1544 | tf_op jit(solution)/shard_map/ppermute | solution.py:244
  8.5 16.3 %collective-permute-start.11 = (f32[2,64]{1,0:T(2,128)S(1)}, f32[2,64]{1,0:T(2,128)S(1)}, u32[]{:S(2)}, u32[]{:S(2)}) collective-permute-start(f32[2,64]{1,0:T(2,128)S(1)} %get-tuple-element.145), channel_id=1, source_target_pairs={{0,16},{1,17},{2,18},{3,19},{4,20},{5,21},{6,22},{7,23},{8,24},{9,... | collective-permute-start | bytes 1544 | tf_op jit(solution)/shard_map/ppermute | solution.py:244
  13.5 13.0 %collective-permute-start.2 = (bf16[208,512]{1,0:T(8,128)(2,1)}, bf16[208,512]{1,0:T(8,128)(2,1)S(1)}, u32[]{:S(2)}, u32[]{:S(2)}) collective-permute-start(bf16[208,512]{1,0:T(8,128)(2,1)} %get-tuple-element.132), channel_id=1, source_target_pairs={{0,6},{1,7},{2,4},{3,5},{4,2},{5,3},{6,0},{7,1},{8,14},{9,15},{10,... | collective-permute-start | bytes 638984 | tf_op jit(solution)/shard_map/ppermute | solution.py:244
  17.5 23.4 %collective-permute-start.3 = (bf16[208,512]{1,0:T(8,128)(2,1)S(1)}, bf16[208,512]{1,0:T(8,128)(2,1)S(1)}, u32[]{:S(2)}, u32[]{:S(2)}) collective-permute-start(bf16[208,512]{1,0:T(8,128)(2,1)S(1)} %get-tuple-element.133.refs_0_), channel_id=1, source_target_pairs={{0,1},{1,0},{2,3},{3,2},{4,5},{5,4},{6,7},{7,6},{8,9},{9,8},{10,11... | collective-permute-start | bytes 638984 | tf_op jit(solution)/shard_map/ppermute | solution.py:244
  24.2 10.4 %collective-permute-start = (bf16[208,512]{1,0:T(8,128)(2,1)}, bf16[208,512]{1,0:T(8,128)(2,1)S(1)}, u32[]{:S(2)}, u32[]{:S(2)}) collective-permute-start(bf16[208,512]{1,0:T(8,128)(2,1)} %get-tuple-element.134), channel_id=1, source_target_pairs={{0,2},{1,3},{2,0},{3,1},{4,6},{5,7},{6,4},{7,5},{8,10},{9,11},{10,... | collective-permute-start | bytes 638984 | tf_op jit(solution)/shard_map/ppermute | solution.py:244
  24.3 13.6 %collective-permute-start.1 = (bf16[208,512]{1,0:T(8,128)(2,1)}, bf16[208,512]{1,0:T(8,128)(2,1)}, u32[]{:S(2)}, u32[]{:S(2)}) collective-permute-start(bf16[208,512]{1,0:T(8,128)(2,1)} %get-tuple-element.135), channel_id=1, source_target_pairs={{0,4},{1,5},{2,6},{3,7},{4,0},{5,1},{6,2},{7,3},{8,12},{9,13},{10,... | collective-permute-start | bytes 638984 | tf_op jit(solution)/shard_map/ppermute | solution.py:244
  24.8 29.4 %collective-permute-start.7 = (bf16[576,512]{1,0:T(8,128)(2,1)S(1)}, bf16[576,512]{1,0:T(8,128)(2,1)}, u32[]{:S(2)}, u32[]{:S(2)}) collective-permute-start(bf16[576,512]{1,0:T(8,128)(2,1)S(1)} %bitcast.137), channel_id=1, source_target_pairs={{0,8},{1,9},{2,10},{3,11},{4,12},{5,13},{6,14},{7,15},{8,0},{9,1},... | collective-permute-start | bytes 1769480 | tf_op jit(solution)/shard_map/ppermute | solution.py:244
  26.6 17.1 %collective-permute-start.6 = (bf16[208,512]{1,0:T(8,128)(2,1)S(1)}, bf16[208,512]{1,0:T(8,128)(2,1)}, u32[]{:S(2)}, u32[]{:S(2)}) collective-permute-start(bf16[208,512]{1,0:T(8,128)(2,1)S(1)} %collective-permute-done.2.refs_3_), channel_id=1, source_target_pairs={{0,1},{1,0},{2,3},{3,2},{4,5},{5,4},{6,7},{7,6},{8,9},{9,8},{10,11... | collective-permute-start | bytes 638984 | tf_op jit(solution)/shard_map/ppermute | solution.py:244
  34.6 11.6 %collective-permute-start.4 = (bf16[208,512]{1,0:T(8,128)(2,1)S(1)}, bf16[208,512]{1,0:T(8,128)(2,1)}, u32[]{:S(2)}, u32[]{:S(2)}) collective-permute-start(bf16[208,512]{1,0:T(8,128)(2,1)S(1)} %collective-permute-done.refs_1_), channel_id=1, source_target_pairs={{0,1},{1,0},{2,3},{3,2},{4,5},{5,4},{6,7},{7,6},{8,9},{9,8},{10,11... | collective-permute-start | bytes 638984 | tf_op jit(solution)/shard_map/ppermute | solution.py:244
  37.8 9.6 %collective-permute-start.5 = (bf16[208,512]{1,0:T(8,128)(2,1)}, bf16[208,512]{1,0:T(8,128)(2,1)}, u32[]{:S(2)}, u32[]{:S(2)}) collective-permute-start(bf16[208,512]{1,0:T(8,128)(2,1)} %collective-permute-done.1.refs_2_), channel_id=1, source_target_pairs={{0,1},{1,0},{2,3},{3,2},{4,5},{5,4},{6,7},{7,6},{8,9},{9,8},{10,11... | collective-permute-start | bytes 638984 | tf_op jit(solution)/shard_map/ppermute | solution.py:244
  40.9 28.5 %collective-permute-start.8 = (bf16[576,512]{1,0:T(8,128)(2,1)S(1)}, bf16[576,512]{1,0:T(8,128)(2,1)}, u32[]{:S(2)}, u32[]{:S(2)}) collective-permute-start(bf16[576,512]{1,0:T(8,128)(2,1)S(1)} %bitcast.136), channel_id=1, source_target_pairs={{0,16},{1,17},{2,18},{3,19},{4,20},{5,21},{6,22},{7,23},{8,24},{9,... | collective-permute-start | bytes 1769480 | tf_op jit(solution)/shard_map/ppermute | solution.py:244
  43.6 25.8 %collective-permute-start.9 = (bf16[576,512]{1,0:T(8,128)(2,1)S(1)}, bf16[576,512]{1,0:T(8,128)(2,1)}, u32[]{:S(2)}, u32[]{:S(2)}) collective-permute-start(bf16[576,512]{1,0:T(8,128)(2,1)S(1)} %bitcast.135), channel_id=1, source_target_pairs={{0,24},{1,25},{2,26},{3,27},{4,28},{5,29},{6,30},{7,31},{8,16},{9,... | collective-permute-start | bytes 1769480 | tf_op jit(solution)/shard_map/ppermute | solution.py:244
  97.6 10.6 %collective-permute-start.21 = (bf16[64,1536]{1,0:T(8,128)(2,1)}, bf16[64,1536]{1,0:T(8,128)(2,1)S(1)}, u32[]{:S(2)}, u32[]{:S(2)}) collective-permute-start(bf16[64,1536]{1,0:T(8,128)(2,1)} %get-tuple-element.62.refs_0_), channel_id=1, source_target_pairs={{0,16},{1,17},{2,18},{3,19},{4,20},{5,21},{6,22},{7,23},{8,24},{9,... | collective-permute-start | bytes 589832 | tf_op jit(solution)/shard_map/ppermute | solution.py:244
  99.3 22.0 %collective-permute-start.23 = (bf16[64,1536]{1,0:T(8,128)(2,1)}, bf16[64,1536]{1,0:T(8,128)(2,1)}, u32[]{:S(2)}, u32[]{:S(2)}) collective-permute-start(bf16[64,1536]{1,0:T(8,128)(2,1)} %get-tuple-element.62.refs_0_), channel_id=1, source_target_pairs={{0,1},{1,0},{2,3},{3,2},{4,5},{5,4},{6,7},{7,6},{8,9},{9,8},{10,11... | collective-permute-start | bytes 589832 | tf_op jit(solution)/shard_map/ppermute | solution.py:244
  104.7 16.6 %collective-permute-start.26 = (bf16[64,1536]{1,0:T(8,128)(2,1)S(1)}, bf16[64,1536]{1,0:T(8,128)(2,1)}, u32[]{:S(2)}, u32[]{:S(2)}) collective-permute-start(bf16[64,1536]{1,0:T(8,128)(2,1)S(1)} %collective-permute-done.22.refs_3_), channel_id=1, source_target_pairs={{0,1},{1,0},{2,3},{3,2},{4,5},{5,4},{6,7},{7,6},{8,9},{9,8},{10,11... | collective-permute-start | bytes 589832 | tf_op jit(solution)/shard_map/ppermute | solution.py:244
  108.2 13.7 %collective-permute-start.25 = (bf16[64,1536]{1,0:T(8,128)(2,1)S(1)}, bf16[64,1536]{1,0:T(8,128)(2,1)}, u32[]{:S(2)}, u32[]{:S(2)}) collective-permute-start(bf16[64,1536]{1,0:T(8,128)(2,1)S(1)} %collective-permute-done.21.refs_2_), channel_id=1, source_target_pairs={{0,1},{1,0},{2,3},{3,2},{4,5},{5,4},{6,7},{7,6},{8,9},{9,8},{10,11... | collective-permute-start | bytes 589832 | tf_op jit(solution)/shard_map/ppermute | solution.py:244
  108.3 13.7 %collective-permute-start.24 = (bf16[64,1536]{1,0:T(8,128)(2,1)S(1)}, bf16[64,1536]{1,0:T(8,128)(2,1)}, u32[]{:S(2)}, u32[]{:S(2)}) collective-permute-start(bf16[64,1536]{1,0:T(8,128)(2,1)S(1)} %collective-permute-done.20.refs_1_), channel_id=1, source_target_pairs={{0,1},{1,0},{2,3},{3,2},{4,5},{5,4},{6,7},{7,6},{8,9},{9,8},{10,11... | collective-permute-start | bytes 589832 | tf_op jit(solution)/shard_map/ppermute | solution.py:244
  121.4 12.0 %collective-permute-start.40 = (bf16[192,128]{1,0:T(8,128)(2,1)S(1)}, bf16[192,128]{1,0:T(8,128)(2,1)}, u32[]{:S(2)}, u32[]{:S(2)}) collective-permute-start(bf16[192,128]{1,0:T(8,128)(2,1)S(1)} %collective-permute-done.36.refs_11_), channel_id=1, source_target_pairs={{0,1},{1,0},{2,3},{3,2},{4,5},{5,4},{6,7},{7,6},{8,9},{9,8},{10,11... | collective-permute-start | bytes 147464 | tf_op jit(solution)/shard_map/ppermute | solution.py:244
  121.9 12.1 %collective-permute-start.39 = (bf16[192,128]{1,0:T(8,128)(2,1)S(1)}, bf16[192,128]{1,0:T(8,128)(2,1)}, u32[]{:S(2)}, u32[]{:S(2)}) collective-permute-start(bf16[192,128]{1,0:T(8,128)(2,1)S(1)} %collective-permute-done.35.refs_10_), channel_id=1, source_target_pairs={{0,1},{1,0},{2,3},{3,2},{4,5},{5,4},{6,7},{7,6},{8,9},{9,8},{10,11... | collective-permute-start | bytes 147464 | tf_op jit(solution)/shard_map/ppermute | solution.py:244
  126.9 9.7 %collective-permute-start.30 = (bf16[64,1536]{1,0:T(8,128)(2,1)}, bf16[64,1536]{1,0:T(8,128)(2,1)S(1)}, u32[]{:S(2)}, u32[]{:S(2)}) collective-permute-start(bf16[64,1536]{1,0:T(8,128)(2,1)} %get-tuple-element.63.refs_0_), channel_id=1, source_target_pairs={{0,1},{1,0},{2,3},{3,2},{4,5},{5,4},{6,7},{7,6},{8,9},{9,8},{10,11... | collective-permute-start | bytes 589832 | tf_op jit(solution)/shard_map/ppermute | solution.py:244
  127.4 10.7 %collective-permute-start.29 = (bf16[64,1536]{1,0:T(8,128)(2,1)}, bf16[64,1536]{1,0:T(8,128)(2,1)S(1)}, u32[]{:S(2)}, u32[]{:S(2)}) collective-permute-start(bf16[64,1536]{1,0:T(8,128)(2,1)} %get-tuple-element.63.refs_0_), channel_id=1, source_target_pairs={{0,24},{1,25},{2,26},{3,27},{4,28},{5,29},{6,30},{7,31},{8,16},{9,... | collective-permute-start | bytes 589832 | tf_op jit(solution)/shard_map/ppermute | solution.py:244
  128.9 23.2 %collective-permute-start.28 = (bf16[64,1536]{1,0:T(8,128)(2,1)}, bf16[64,1536]{1,0:T(8,128)(2,1)}, u32[]{:S(2)}, u32[]{:S(2)}) collective-permute-start(bf16[64,1536]{1,0:T(8,128)(2,1)} %get-tuple-element.63.refs_0_), channel_id=1, source_target_pairs={{0,16},{1,17},{2,18},{3,19},{4,20},{5,21},{6,22},{7,23},{8,24},{9,... | collective-permute-start | bytes 589832 | tf_op jit(solution)/shard_map/ppermute | solution.py:244
  133.3 44.5 %collective-permute-start.57 = (bf16[576,512]{1,0:T(8,128)(2,1)}, bf16[576,512]{1,0:T(8,128)(2,1)}, u32[]{:S(2)}, u32[]{:S(2)}) collective-permute-start(bf16[576,512]{1,0:T(8,128)(2,1)} %bitcast.140), channel_id=1, source_target_pairs={{0,16},{1,17},{2,18},{3,19},{4,20},{5,21},{6,22},{7,23},{8,24},{9,... | collective-permute-start | bytes 1769480 | tf_op jit(solution)/shard_map/ppermute | solution.py:244
  135.2 44.1 %collective-permute-start.58 = (bf16[576,512]{1,0:T(8,128)(2,1)}, bf16[576,512]{1,0:T(8,128)(2,1)}, u32[]{:S(2)}, u32[]{:S(2)}) collective-permute-start(bf16[576,512]{1,0:T(8,128)(2,1)} %bitcast.139), channel_id=1, source_target_pairs={{0,24},{1,25},{2,26},{3,27},{4,28},{5,29},{6,30},{7,31},{8,16},{9,... | collective-permute-start | bytes 1769480 | tf_op jit(solution)/shard_map/ppermute | solution.py:244
  136.6 52.0 %collective-permute-start.56 = (bf16[576,512]{1,0:T(8,128)(2,1)}, bf16[576,512]{1,0:T(8,128)(2,1)}, u32[]{:S(2)}, u32[]{:S(2)}) collective-permute-start(bf16[576,512]{1,0:T(8,128)(2,1)} %bitcast.138), channel_id=1, source_target_pairs={{0,8},{1,9},{2,10},{3,11},{4,12},{5,13},{6,14},{7,15},{8,0},{9,1},... | collective-permute-start | bytes 1769480 | tf_op jit(solution)/shard_map/ppermute | solution.py:244
  138.1 30.6 %collective-permute-start.27 = (bf16[64,1536]{1,0:T(8,128)(2,1)}, bf16[64,1536]{1,0:T(8,128)(2,1)}, u32[]{:S(2)}, u32[]{:S(2)}) collective-permute-start(bf16[64,1536]{1,0:T(8,128)(2,1)} %get-tuple-element.63.refs_0_), channel_id=1, source_target_pairs={{0,8},{1,9},{2,10},{3,11},{4,12},{5,13},{6,14},{7,15},{8,0},{9,1},... | collective-permute-start | bytes 589832 | tf_op jit(solution)/shard_map/ppermute | solution.py:244
  152.1 16.5 %collective-permute-start.33 = (bf16[64,1536]{1,0:T(8,128)(2,1)S(1)}, bf16[64,1536]{1,0:T(8,128)(2,1)S(1)}, u32[]{:S(2)}, u32[]{:S(2)}) collective-permute-start(bf16[64,1536]{1,0:T(8,128)(2,1)S(1)} %collective-permute-done.29.refs_3_), channel_id=1, source_target_pairs={{0,1},{1,0},{2,3},{3,2},{4,5},{5,4},{6,7},{7,6},{8,9},{9,8},{10,11... | collective-permute-start | bytes 589832 | tf_op jit(solution)/shard_map/ppermute | solution.py:244
  177.3 10.8 %collective-permute-start.50 = (bf16[64,1536]{1,0:T(8,128)(2,1)S(1)}, bf16[64,1536]{1,0:T(8,128)(2,1)S(1)}, u32[]{:S(2)}, u32[]{:S(2)}) collective-permute-start(bf16[64,1536]{1,0:T(8,128)(2,1)S(1)} %get-tuple-element.68.refs_0_.refs_8_), channel_id=1, source_target_pairs={{0,16},{1,17},{2,18},{3,19},{4,20},{5,21},{6,22},{7,23},{8,24},{9,... | collective-permute-start | bytes 589832 | tf_op jit(solution)/shard_map/ppermute | solution.py:244
  177.8 10.3 %collective-permute-start.49 = (bf16[64,1536]{1,0:T(8,128)(2,1)S(1)}, bf16[64,1536]{1,0:T(8,128)(2,1)S(1)}, u32[]{:S(2)}, u32[]{:S(2)}) collective-permute-start(bf16[64,1536]{1,0:T(8,128)(2,1)S(1)} %get-tuple-element.68.refs_0_.refs_8_), channel_id=1, source_target_pairs={{0,8},{1,9},{2,10},{3,11},{4,12},{5,13},{6,14},{7,15},{8,0},{9,1},... | collective-permute-start | bytes 589832 | tf_op jit(solution)/shard_map/ppermute | solution.py:244
  179.3 11.1 %collective-permute-start.52 = (bf16[64,1536]{1,0:T(8,128)(2,1)S(1)}, bf16[64,1536]{1,0:T(8,128)(2,1)S(1)}, u32[]{:S(2)}, u32[]{:S(2)}) collective-permute-start(bf16[64,1536]{1,0:T(8,128)(2,1)S(1)} %get-tuple-element.68.refs_0_.refs_8_), channel_id=1, source_target_pairs={{0,1},{1,0},{2,3},{3,2},{4,5},{5,4},{6,7},{7,6},{8,9},{9,8},{10,11... | collective-permute-start | bytes 589832 | tf_op jit(solution)/shard_map/ppermute | solution.py:244
  193.7 10.4 %collective-permute-start.60 = (bf16[64,1536]{1,0:T(8,128)(2,1)S(1)}, bf16[64,1536]{1,0:T(8,128)(2,1)S(1)}, u32[]{:S(2)}, u32[]{:S(2)}) collective-permute-start(bf16[64,1536]{1,0:T(8,128)(2,1)S(1)} %get-tuple-element.71.refs_0_.refs_8_), channel_id=1, source_target_pairs={{0,16},{1,17},{2,18},{3,19},{4,20},{5,21},{6,22},{7,23},{8,24},{9,... | collective-permute-start | bytes 589832 | tf_op jit(solution)/shard_map/ppermute | solution.py:244
  194.2 10.0 %collective-permute-start.59 = (bf16[64,1536]{1,0:T(8,128)(2,1)S(1)}, bf16[64,1536]{1,0:T(8,128)(2,1)S(1)}, u32[]{:S(2)}, u32[]{:S(2)}) collective-permute-start(bf16[64,1536]{1,0:T(8,128)(2,1)S(1)} %get-tuple-element.71.refs_0_.refs_8_), channel_id=1, source_target_pairs={{0,8},{1,9},{2,10},{3,11},{4,12},{5,13},{6,14},{7,15},{8,0},{9,1},... | collective-permute-start | bytes 589832 | tf_op jit(solution)/shard_map/ppermute | solution.py:244
  195.7 9.6 %collective-permute-start.62 = (bf16[64,1536]{1,0:T(8,128)(2,1)S(1)}, bf16[64,1536]{1,0:T(8,128)(2,1)S(1)}, u32[]{:S(2)}, u32[]{:S(2)}) collective-permute-start(bf16[64,1536]{1,0:T(8,128)(2,1)S(1)} %get-tuple-element.71.refs_0_.refs_8_), channel_id=1, source_target_pairs={{0,1},{1,0},{2,3},{3,2},{4,5},{5,4},{6,7},{7,6},{8,9},{9,8},{10,11... | collective-permute-start | bytes 589832 | tf_op jit(solution)/shard_map/ppermute | solution.py:244
  204.7 14.7 %collective-permute-start.41 = (bf16[64,384]{1,0:T(8,128)(2,1)S(1)}, bf16[64,384]{1,0:T(8,128)(2,1)S(1)}, u32[]{:S(2)}, u32[]{:S(2)}) collective-permute-start(bf16[64,384]{1,0:T(8,128)(2,1)S(1)} %get-tuple-element.64), channel_id=1, source_target_pairs={{0,0},{1,1},{2,8},{3,9},{4,16},{5,17},{6,24},{7,25},{8,2},{9,3},{1... | collective-permute-start | bytes 147464 | tf_op jit(solution)/shard_map/ppermute | solution.py:244
  210.0 21.2 %collective-permute-start.68 = (bf16[64,1536]{1,0:T(8,128)(2,1)S(1)}, bf16[64,1536]{1,0:T(8,128)(2,1)S(1)}, u32[]{:S(2)}, u32[]{:S(2)}) collective-permute-start(bf16[64,1536]{1,0:T(8,128)(2,1)S(1)} %get-tuple-element.74.refs_0_.refs_8_), channel_id=1, source_target_pairs={{0,24},{1,25},{2,26},{3,27},{4,28},{5,29},{6,30},{7,31},{8,16},{9,... | collective-permute-start | bytes 589832 | tf_op jit(solution)/shard_map/ppermute | solution.py:244
  214.7 17.1 %collective-permute-start.67 = (bf16[64,1536]{1,0:T(8,128)(2,1)S(1)}, bf16[64,1536]{1,0:T(8,128)(2,1)S(1)}, u32[]{:S(2)}, u32[]{:S(2)}) collective-permute-start(bf16[64,1536]{1,0:T(8,128)(2,1)S(1)} %get-tuple-element.74.refs_0_.refs_8_), channel_id=1, source_target_pairs={{0,16},{1,17},{2,18},{3,19},{4,20},{5,21},{6,22},{7,23},{8,24},{9,... | collective-permute-start | bytes 589832 | tf_op jit(solution)/shard_map/ppermute | solution.py:244
  215.8 16.0 %collective-permute-start.66 = (bf16[64,1536]{1,0:T(8,128)(2,1)S(1)}, bf16[64,1536]{1,0:T(8,128)(2,1)S(1)}, u32[]{:S(2)}, u32[]{:S(2)}) collective-permute-start(bf16[64,1536]{1,0:T(8,128)(2,1)S(1)} %get-tuple-element.74.refs_0_.refs_8_), channel_id=1, source_target_pairs={{0,8},{1,9},{2,10},{3,11},{4,12},{5,13},{6,14},{7,15},{8,0},{9,1},... | collective-permute-start | bytes 589832 | tf_op jit(solution)/shard_map/ppermute | solution.py:244
  218.7 13.5 %collective-permute-start.97 = (bf16[592,128]{1,0:T(8,128)(2,1)S(1)}, bf16[592,128]{1,0:T(8,128)(2,1)S(1)}, u32[]{:S(2)}, u32[]{:S(2)}) collective-permute-start(bf16[592,128]{1,0:T(8,128)(2,1)S(1)} %get-tuple-element.103), channel_id=1, source_target_pairs={{0,2},{1,3},{2,0},{3,1},{4,6},{5,7},{6,4},{7,5},{8,10},{9,11},{10,... | collective-permute-start | bytes 454664 | tf_op jit(solution)/shard_map/ppermute | solution.py:244
  231.2 15.2 %collective-permute-start.69 = (bf16[64,1536]{1,0:T(8,128)(2,1)S(1)}, bf16[64,1536]{1,0:T(8,128)(2,1)S(1)}, u32[]{:S(2)}, u32[]{:S(2)}) collective-permute-start(bf16[64,1536]{1,0:T(8,128)(2,1)S(1)} %get-tuple-element.74.refs_0_.refs_8_), channel_id=1, source_target_pairs={{0,1},{1,0},{2,3},{3,2},{4,5},{5,4},{6,7},{7,6},{8,9},{9,8},{10,11... | collective-permute-start | bytes 589832 | tf_op jit(solution)/shard_map/ppermute | solution.py:244
  231.2 15.2 %collective-permute-start.72 = (bf16[64,1536]{1,0:T(8,128)(2,1)S(1)}, bf16[64,1536]{1,0:T(8,128)(2,1)S(1)}, u32[]{:S(2)}, u32[]{:S(2)}) collective-permute-start(bf16[64,1536]{1,0:T(8,128)(2,1)S(1)} %collective-permute-done.68.refs_3_), channel_id=1, source_target_pairs={{0,1},{1,0},{2,3},{3,2},{4,5},{5,4},{6,7},{7,6},{8,9},{9,8},{10,11... | collective-permute-start | bytes 589832 | tf_op jit(solution)/shard_map/ppermute | solution.py:244
  231.7 15.6 %collective-permute-start.71 = (bf16[64,1536]{1,0:T(8,128)(2,1)S(1)}, bf16[64,1536]{1,0:T(8,128)(2,1)S(1)}, u32[]{:S(2)}, u32[]{:S(2)}) collective-permute-start(bf16[64,1536]{1,0:T(8,128)(2,1)S(1)} %collective-permute-done.67.refs_2_), channel_id=1, source_target_pairs={{0,1},{1,0},{2,3},{3,2},{4,5},{5,4},{6,7},{7,6},{8,9},{9,8},{10,11... | collective-permute-start | bytes 589832 | tf_op jit(solution)/shard_map/ppermute | solution.py:244
  231.8 19.0 %collective-permute-start.70 = (bf16[64,1536]{1,0:T(8,128)(2,1)S(1)}, bf16[64,1536]{1,0:T(8,128)(2,1)S(1)}, u32[]{:S(2)}, u32[]{:S(2)}) collective-permute-start(bf16[64,1536]{1,0:T(8,128)(2,1)S(1)} %collective-permute-done.66.refs_1_), channel_id=1, source_target_pairs={{0,1},{1,0},{2,3},{3,2},{4,5},{5,4},{6,7},{7,6},{8,9},{9,8},{10,11... | collective-permute-start | bytes 589832 | tf_op jit(solution)/shard_map/ppermute | solution.py:244
  232.2 10.7 %collective-permute-start.98 = (bf16[592,128]{1,0:T(8,128)(2,1)S(1)}, bf16[592,128]{1,0:T(8,128)(2,1)S(1)}, u32[]{:S(2)}, u32[]{:S(2)}) collective-permute-start(bf16[592,128]{1,0:T(8,128)(2,1)S(1)} %get-tuple-element.104), channel_id=1, source_target_pairs={{0,4},{1,5},{2,6},{3,7},{4,0},{5,1},{6,2},{7,3},{8,12},{9,13},{10,... | collective-permute-start | bytes 454664 | tf_op jit(solution)/shard_map/ppermute | solution.py:244
  242.9 12.6 %collective-permute-start.99 = (bf16[592,128]{1,0:T(8,128)(2,1)S(1)}, bf16[592,128]{1,0:T(8,128)(2,1)S(1)}, u32[]{:S(2)}, u32[]{:S(2)}) collective-permute-start(bf16[592,128]{1,0:T(8,128)(2,1)S(1)} %get-tuple-element.105), channel_id=1, source_target_pairs={{0,6},{1,7},{2,4},{3,5},{4,2},{5,3},{6,0},{7,1},{8,14},{9,15},{10,... | collective-permute-start | bytes 454664 | tf_op jit(solution)/shard_map/ppermute | solution.py:244
  246.4 9.9 %collective-permute-start.94 = (bf16[592,128]{1,0:T(8,128)(2,1)S(1)}, bf16[592,128]{1,0:T(8,128)(2,1)S(1)}, u32[]{:S(2)}, u32[]{:S(2)}) collective-permute-start(bf16[592,128]{1,0:T(8,128)(2,1)S(1)} %get-tuple-element.97), channel_id=1, source_target_pairs={{0,2},{1,3},{2,0},{3,1},{4,6},{5,7},{6,4},{7,5},{8,10},{9,11},{10,... | collective-permute-start | bytes 454664 | tf_op jit(solution)/shard_map/ppermute | solution.py:244
  246.4 16.8 %collective-permute-start.95 = (bf16[592,128]{1,0:T(8,128)(2,1)S(1)}, bf16[592,128]{1,0:T(8,128)(2,1)S(1)}, u32[]{:S(2)}, u32[]{:S(2)}) collective-permute-start(bf16[592,128]{1,0:T(8,128)(2,1)S(1)} %get-tuple-element.98), channel_id=1, source_target_pairs={{0,4},{1,5},{2,6},{3,7},{4,0},{5,1},{6,2},{7,3},{8,12},{9,13},{10,... | collective-permute-start | bytes 454664 | tf_op jit(solution)/shard_map/ppermute | solution.py:244
  247.3 15.9 %collective-permute-start.96 = (bf16[592,128]{1,0:T(8,128)(2,1)S(1)}, bf16[592,128]{1,0:T(8,128)(2,1)S(1)}, u32[]{:S(2)}, u32[]{:S(2)}) collective-permute-start(bf16[592,128]{1,0:T(8,128)(2,1)S(1)} %get-tuple-element.99), channel_id=1, source_target_pairs={{0,6},{1,7},{2,4},{3,5},{4,2},{5,3},{6,0},{7,1},{8,14},{9,15},{10,... | collective-permute-start | bytes 454664 | tf_op jit(solution)/shard_map/ppermute | solution.py:244
  250.8 21.4 %collective-permute-start.91 = (bf16[592,128]{1,0:T(8,128)(2,1)S(1)}, bf16[592,128]{1,0:T(8,128)(2,1)S(1)}, u32[]{:S(2)}, u32[]{:S(2)}) collective-permute-start(bf16[592,128]{1,0:T(8,128)(2,1)S(1)} %get-tuple-element.91), channel_id=1, source_target_pairs={{0,2},{1,3},{2,0},{3,1},{4,6},{5,7},{6,4},{7,5},{8,10},{9,11},{10,... | collective-permute-start | bytes 454664 | tf_op jit(solution)/shard_map/ppermute | solution.py:244
  255.5 27.0 %collective-permute-start.92 = (bf16[592,128]{1,0:T(8,128)(2,1)S(1)}, bf16[592,128]{1,0:T(8,128)(2,1)S(1)}, u32[]{:S(2)}, u32[]{:S(2)}) collective-permute-start(bf16[592,128]{1,0:T(8,128)(2,1)S(1)} %get-tuple-element.92), channel_id=1, source_target_pairs={{0,4},{1,5},{2,6},{3,7},{4,0},{5,1},{6,2},{7,3},{8,12},{9,13},{10,... | collective-permute-start | bytes 454664 | tf_op jit(solution)/shard_map/ppermute | solution.py:244
  256.4 26.1 %collective-permute-start.93 = (bf16[592,128]{1,0:T(8,128)(2,1)S(1)}, bf16[592,128]{1,0:T(8,128)(2,1)S(1)}, u32[]{:S(2)}, u32[]{:S(2)}) collective-permute-start(bf16[592,128]{1,0:T(8,128)(2,1)S(1)} %get-tuple-element.93), channel_id=1, source_target_pairs={{0,6},{1,7},{2,4},{3,5},{4,2},{5,3},{6,0},{7,1},{8,14},{9,15},{10,... | collective-permute-start | bytes 454664 | tf_op jit(solution)/shard_map/ppermute | solution.py:244
  263.2 19.3 %collective-permute-start.88 = (bf16[592,128]{1,0:T(8,128)(2,1)S(1)}, bf16[592,128]{1,0:T(8,128)(2,1)S(1)}, u32[]{:S(2)}, u32[]{:S(2)}) collective-permute-start(bf16[592,128]{1,0:T(8,128)(2,1)S(1)} %get-tuple-element.85), channel_id=1, source_target_pairs={{0,2},{1,3},{2,0},{3,1},{4,6},{5,7},{6,4},{7,5},{8,10},{9,11},{10,... | collective-permute-start | bytes 454664 | tf_op jit(solution)/shard_map/ppermute | solution.py:244
  263.2 25.7 %collective-permute-start.89 = (bf16[592,128]{1,0:T(8,128)(2,1)S(1)}, bf16[592,128]{1,0:T(8,128)(2,1)S(1)}, u32[]{:S(2)}, u32[]{:S(2)}) collective-permute-start(bf16[592,128]{1,0:T(8,128)(2,1)S(1)} %get-tuple-element.86), channel_id=1, source_target_pairs={{0,4},{1,5},{2,6},{3,7},{4,0},{5,1},{6,2},{7,3},{8,12},{9,13},{10,... | collective-permute-start | bytes 454664 | tf_op jit(solution)/shard_map/ppermute | solution.py:244
  272.2 16.7 %collective-permute-start.90 = (bf16[592,128]{1,0:T(8,128)(2,1)S(1)}, bf16[592,128]{1,0:T(8,128)(2,1)S(1)}, u32[]{:S(2)}, u32[]{:S(2)}) collective-permute-start(bf16[592,128]{1,0:T(8,128)(2,1)S(1)} %get-tuple-element.87), channel_id=1, source_target_pairs={{0,6},{1,7},{2,4},{3,5},{4,2},{5,3},{6,0},{7,1},{8,14},{9,15},{10,... | collective-permute-start | bytes 454664 | tf_op jit(solution)/shard_map/ppermute | solution.py:244
  282.5 11.9 %collective-permute-start.46 = (bf16[64,384]{1,0:T(8,128)(2,1)S(1)}, bf16[64,384]{1,0:T(8,128)(2,1)S(1)}, u32[]{:S(2)}, u32[]{:S(2)}) collective-permute-start(bf16[64,384]{1,0:T(8,128)(2,1)S(1)} %collective-permute-done.42.refs_1_), channel_id=1, source_target_pairs={{0,1},{1,0},{2,3},{3,2},{4,5},{5,4},{6,7},{7,6},{8,9},{9,8},{10,11... | collective-permute-start | bytes 147464 | tf_op jit(solution)/shard_map/ppermute | solution.py:244
  291.1 13.3 %collective-permute-start.74 = (bf16[64,1536]{1,0:T(8,128)(2,1)S(1)}, bf16[64,1536]{1,0:T(8,128)(2,1)S(1)}, u32[]{:S(2)}, u32[]{:S(2)}) collective-permute-start(bf16[64,1536]{1,0:T(8,128)(2,1)S(1)} %get-tuple-element.77.refs_0_.refs_8_), channel_id=1, source_target_pairs={{0,16},{1,17},{2,18},{3,19},{4,20},{5,21},{6,22},{7,23},{8,24},{9,... | collective-permute-start | bytes 589832 | tf_op jit(solution)/shard_map/ppermute | solution.py:244
  294.4 11.4 %collective-permute-start.73 = (bf16[64,1536]{1,0:T(8,128)(2,1)S(1)}, bf16[64,1536]{1,0:T(8,128)(2,1)S(1)}, u32[]{:S(2)}, u32[]{:S(2)}) collective-permute-start(bf16[64,1536]{1,0:T(8,128)(2,1)S(1)} %get-tuple-element.77.refs_0_.refs_8_), channel_id=1, source_target_pairs={{0,8},{1,9},{2,10},{3,11},{4,12},{5,13},{6,14},{7,15},{8,0},{9,1},... | collective-permute-start | bytes 589832 | tf_op jit(solution)/shard_map/ppermute | solution.py:244
  295.9 9.9 %collective-permute-start.102 = (bf16[592,128]{1,0:T(8,128)(2,1)S(1)}, bf16[592,128]{1,0:T(8,128)(2,1)S(1)}, u32[]{:S(2)}, u32[]{:S(2)}) collective-permute-start(bf16[592,128]{1,0:T(8,128)(2,1)S(1)} %get-tuple-element.113), channel_id=1, source_target_pairs={{0,24},{1,25},{2,26},{3,27},{4,28},{5,29},{6,30},{7,31},{8,16},{9,... | collective-permute-start | bytes 454664 | tf_op jit(solution)/shard_map/ppermute | solution.py:244
  297.5 11.9 %collective-permute-start.101 = (bf16[592,128]{1,0:T(8,128)(2,1)S(1)}, bf16[592,128]{1,0:T(8,128)(2,1)S(1)}, u32[]{:S(2)}, u32[]{:S(2)}) collective-permute-start(bf16[592,128]{1,0:T(8,128)(2,1)S(1)} %get-tuple-element.140), channel_id=1, source_target_pairs={{0,16},{1,17},{2,18},{3,19},{4,20},{5,21},{6,22},{7,23},{8,24},{9,... | collective-permute-start | bytes 454664 | tf_op jit(solution)/shard_map/ppermute | solution.py:244
  298.4 13.8 %collective-permute-start.79 = (bf16[64,1536]{1,0:T(8,128)(2,1)S(1)}, bf16[64,1536]{1,0:T(8,128)(2,1)S(1)}, u32[]{:S(2)}, u32[]{:S(2)}) collective-permute-start(bf16[64,1536]{1,0:T(8,128)(2,1)S(1)} %collective-permute-done.75.refs_3_), channel_id=1, source_target_pairs={{0,1},{1,0},{2,3},{3,2},{4,5},{5,4},{6,7},{7,6},{8,9},{9,8},{10,11... | collective-permute-start | bytes 589832 | tf_op jit(solution)/shard_map/ppermute | solution.py:244
  312.2 19.3 %collective-permute-start.106 = (bf16[592,128]{1,0:T(8,128)(2,1)S(1)}, bf16[592,128]{1,0:T(8,128)(2,1)S(1)}, u32[]{:S(2)}, u32[]{:S(2)}) collective-permute-start(bf16[592,128]{1,0:T(8,128)(2,1)S(1)} %collective-permute-done.102.refs_3_), channel_id=1, source_target_pairs={{0,1},{1,0},{2,3},{3,2},{4,5},{5,4},{6,7},{7,6},{8,9},{9,8},{10,11... | collective-permute-start | bytes 454664 | tf_op jit(solution)/shard_map/ppermute | solution.py:244
  312.7 19.3 %collective-permute-start.105 = (bf16[592,128]{1,0:T(8,128)(2,1)S(1)}, bf16[592,128]{1,0:T(8,128)(2,1)S(1)}, u32[]{:S(2)}, u32[]{:S(2)}) collective-permute-start(bf16[592,128]{1,0:T(8,128)(2,1)S(1)} %collective-permute-done.101.refs_2_), channel_id=1, source_target_pairs={{0,1},{1,0},{2,3},{3,2},{4,5},{5,4},{6,7},{7,6},{8,9},{9,8},{10,11... | collective-permute-start | bytes 454664 | tf_op jit(solution)/shard_map/ppermute | solution.py:244
  312.7 20.2 %collective-permute-start.104 = (bf16[592,128]{1,0:T(8,128)(2,1)S(1)}, bf16[592,128]{1,0:T(8,128)(2,1)S(1)}, u32[]{:S(2)}, u32[]{:S(2)}) collective-permute-start(bf16[592,128]{1,0:T(8,128)(2,1)S(1)} %collective-permute-done.100.refs_1_), channel_id=1, source_target_pairs={{0,1},{1,0},{2,3},{3,2},{4,5},{5,4},{6,7},{7,6},{8,9},{9,8},{10,11... | collective-permute-start | bytes 454664 | tf_op jit(solution)/shard_map/ppermute | solution.py:244
  315.4 10.1 %collective-permute-start.81 = (bf16[64,384]{1,0:T(8,128)(2,1)S(1)}, bf16[64,384]{1,0:T(8,128)(2,1)S(1)}, u32[]{:S(2)}, u32[]{:S(2)}) collective-permute-start(bf16[64,384]{1,0:T(8,128)(2,1)S(1)} %get-tuple-element.79), channel_id=1, source_target_pairs={{0,2},{1,3},{2,10},{3,11},{4,18},{5,19},{6,26},{7,27},{8,0},{9,1},... | collective-permute-start | bytes 147464 | tf_op jit(solution)/shard_map/ppermute | solution.py:244
  (64 other events, 343.2 us)
